TPU v7x, 32 devices: a whole 2x2x4 slice. The times are simulated.
32 devices in a mesh: wide: 8 (over y, x, core), narrow: 4 (over z).
Axes of the slice: x: 2, y: 2, z: 4, core: 2. Of those that a mesh axis runs over, the one named last changes fastest.
Arguments:
- volume: bfloat16 [32, 32, 16, 128], P(None, 'wide', 'narrow'), may hold values from -6 to 6
- cotangent: bfloat16 [32, 32, 16, 128], P(None, 'wide', 'narrow'), may hold values from -6 to 6
- conv_first: bfloat16 [3, 3, 3, 32, 32], replicated, may hold values from -0.21875 to 0.21875
- conv_second: bfloat16 [3, 3, 3, 32, 64], replicated, may hold values from -0.21875 to 0.21875
- conv_bottom: bfloat16 [3, 3, 3, 64, 128], replicated, may hold values from -0.3125 to 0.3125
- lift_weight: bfloat16 [64, 128], replicated, may hold values from -2 to 2
- conv_decode: bfloat16 [3, 3, 3, 64, 32], replicated, may hold values from -0.15625 to 0.15625
- conv_final: bfloat16 [3, 3, 3, 32, 32], replicated, may hold values from -0.21875 to 0.21875
Outputs:
- features_out: bfloat16 [32, 32, 16, 128], P(None, 'wide', 'narrow')
- input_grad: bfloat16 [32, 32, 16, 128], P(None, 'wide', 'narrow')
All inputs are finite; a program needn't handle non-finite values.
Results may differ from a plain program's by a relative error of at most 0.013.
Values may be sent and summed in bfloat16 or wider, within the bound.
A program may use at most 64 MiB of HBM per device.

v0:
```python
import jax
import jax.numpy as jnp
from jax import lax
from jax.sharding import PartitionSpec as P


def extended(cells, sides, width):
    for axis, dim in sides:
        count = lax.axis_size(axis)
        ends = count - 1
        head = lax.slice_in_dim(cells, 0, width, axis=dim)
        tail = lax.slice_in_dim(cells, cells.shape[dim] - width, cells.shape[dim], axis=dim)
        cells = jnp.concatenate(
            [
                lax.ppermute(tail, axis, [(i, (i + 1) % count) for i in range(ends)]),
                cells,
                lax.ppermute(head, axis, [((i + 1) % count, i) for i in range(ends)]),
            ],
            axis=dim,
        )
    return cells


def conv_valid(padded, kernel):
    padded = jnp.pad(padded, ((0, 0), (0, 0), (0, 0), (1, 1)))
    out = lax.conv_general_dilated(
        padded[None],
        kernel,
        (1, 1, 1),
        "VALID",
        dimension_numbers=("NCDHW", "DHWIO", "NCDHW"),
        preferred_element_type=jnp.float32,
    )
    return out[0]


def flipped(kernel):
    return jnp.flip(kernel, (0, 1, 2)).transpose(0, 1, 2, 4, 3)


def blocks(field):
    chans, xs, ys, zs = field.shape
    return field.astype(jnp.float32).reshape(chans, xs // 2, 2, ys // 2, 2, zs // 2, 2)


def pool_mean(field):
    return jnp.mean(blocks(field), axis=(2, 4, 6))


def pool_sum(field):
    return jnp.sum(blocks(field), axis=(2, 4, 6))


def upsample(field):
    return jnp.repeat(jnp.repeat(jnp.repeat(field, 2, 1), 2, 2), 2, 3)


def silu(value):
    return value * jax.nn.sigmoid(value)


def slope(value):
    sigma = jax.nn.sigmoid(value)
    return sigma * (1.0 + value * (1.0 - sigma))


def pointwise(matrix, field):
    chans, xs, ys, zs = field.shape
    flat = field.reshape(chans, xs * ys * zs)
    out = jnp.dot(matrix, flat, preferred_element_type=jnp.float32)
    return out.reshape(matrix.shape[0], xs, ys, zs)


def shards(
    volume, cotangent, conv_first, conv_second, conv_bottom, lift_weight, conv_decode, conv_final
):
    bf = jnp.bfloat16
    f32 = jnp.float32
    edged = extended(volume, (("wide", 1), ("narrow", 2)), 1)
    pre_first = conv_valid(edged, conv_first)
    hidden_first = silu(pre_first).astype(bf)
    pooled_first = pool_mean(hidden_first).astype(bf)
    edged_second = extended(pooled_first, (("wide", 1), ("narrow", 2)), 1)
    pre_second = conv_valid(edged_second, conv_second)
    hidden_second = silu(pre_second).astype(bf)
    pooled_second = pool_mean(hidden_second).astype(bf)
    edged_bottom = extended(pooled_second, (("wide", 1), ("narrow", 2)), 1)
    pre_bottom = conv_valid(edged_bottom, conv_bottom)
    hidden_bottom = silu(pre_bottom).astype(bf)
    joined_second = (
        upsample(pointwise(lift_weight, hidden_bottom)) + hidden_second.astype(f32)
    ).astype(bf)
    edged_decode = extended(joined_second, (("wide", 1), ("narrow", 2)), 1)
    pre_decode = conv_valid(edged_decode, conv_decode)
    hidden_decode = silu(pre_decode).astype(bf)
    joined_first = (upsample(hidden_decode).astype(f32) + hidden_first.astype(f32)).astype(bf)
    joined_wide = extended(joined_first, (("wide", 1), ("narrow", 2)), 1)
    features_out = conv_valid(joined_wide, conv_final).astype(bf)
    edged_grad = extended(cotangent, (("wide", 1), ("narrow", 2)), 1)
    grad_joined = conv_valid(edged_grad, flipped(conv_final)).astype(bf)
    grad_decode = (pool_sum(grad_joined) * slope(pre_decode)).astype(bf)
    edged_decode_grad = extended(grad_decode, (("wide", 1), ("narrow", 2)), 1)
    grad_second_up = conv_valid(edged_decode_grad, flipped(conv_decode)).astype(bf)
    grad_lift = pool_sum(grad_second_up).astype(bf)
    grad_bottom = (pointwise(lift_weight.T, grad_lift) * slope(pre_bottom)).astype(bf)
    edged_bottom_grad = extended(grad_bottom, (("wide", 1), ("narrow", 2)), 1)
    grad_pool_second = conv_valid(edged_bottom_grad, flipped(conv_bottom))
    grad_second = (
        (grad_second_up.astype(f32) + upsample(grad_pool_second) / 8.0) * slope(pre_second)
    ).astype(bf)
    edged_second_grad = extended(grad_second, (("wide", 1), ("narrow", 2)), 1)
    grad_pool_first = conv_valid(edged_second_grad, flipped(conv_second))
    grad_first = (
        (grad_joined.astype(f32) + upsample(grad_pool_first) / 8.0) * slope(pre_first)
    ).astype(bf)
    edged_first_grad = extended(grad_first, (("wide", 1), ("narrow", 2)), 1)
    input_grad = conv_valid(edged_first_grad, flipped(conv_first)).astype(bf)
    return (features_out, input_grad)


def solution(mesh):
    placed = (
        P(None, "wide", "narrow", None),
        P(None, "wide", "narrow", None),
        P(),
        P(),
        P(),
        P(),
        P(),
        P(),
    )
    return jax.shard_map(
        shards,
        mesh=mesh,
        in_specs=placed,
        out_specs=(P(None, "wide", "narrow", None), P(None, "wide", "narrow", None)),
        check_vma=False,
    )
```

profile of v0, /device:TPU:4, one launch (start us, length us, event | category | flops | bytes accessed | tf_op | source)
XLA Modules:
  0.0 217.3 jit_solution(108546529806526461)
XLA Ops:
  1.5 2.8 %collective-permute-start.1 = (bf16[32,1,4,128]{3,2,1,0:T(4,128)(2,1)S(1)}, bf16[32,1,4,128]{3,2,1,0:T(4,128)(2,1)S(1)}, u32[]{:S(2)}, u32[]{:S(2)}) collective-permute-start(bf16[32,1,4,128]{3,2,1,0:T(4,128)(2,1)S(1)} %get-tuple-element.38), channel_id=1, source_target_pairs={{4,0},{8,4},{12,8},{16,12},{20,16},{24,20},{28,24},{5,1},{9,5},{13... | collective-permute-start | bytes 98312 | tf_op jit(solution)/shard_map/ppermute | solution.py:17
  4.3 1.9 collective-permute-start
  7.0 4.5 %collective-permute-start.21 = (bf16[32,1,4,128]{3,2,1,0:T(4,128)(2,1)S(1)}, bf16[32,1,4,128]{3,2,1,0:T(4,128)(2,1)S(1)}, u32[]{:S(2)}, u32[]{:S(2)}) collective-permute-start(bf16[32,1,4,128]{3,2,1,0:T(4,128)(2,1)S(1)} %get-tuple-element.32), channel_id=1, source_target_pairs={{4,0},{8,4},{12,8},{16,12},{20,16},{24,20},{28,24},{5,1},{9,5},{13... | collective-permute-start | bytes 98312 | tf_op jit(solution)/shard_map/ppermute | solution.py:17
  11.6 1.9 collective-permute-start.20
  14.7 3.5 %collective-permute-start.2 = (bf16[32,6,1,128]{3,2,1,0:T(2,128)(2,1)S(1)}, bf16[32,6,1,128]{3,2,1,0:T(2,128)(2,1)S(1)}, u32[]{:S(2)}, u32[]{:S(2)}) collective-permute-start(bf16[32,6,1,128]{3,2,1,0:T(2,128)(2,1)S(1)} %get-tuple-element.26), channel_id=1, source_target_pairs={{0,1},{1,2},{2,3},{4,5},{5,6},{6,7},{8,9},{9,10},{10,11},{12,13},{... | collective-permute-start | bytes 147464 | tf_op jit(solution)/shard_map/ppermute | solution.py:15
  18.2 1.3 collective-permute-start.3
  20.4 4.3 %collective-permute-done.3 = bf16[32,6,1,128]{3,2,1,0:T(2,128)(2,1)S(1)} collective-permute-done((bf16[32,6,1,128]{3,2,1,0:T(2,128)(2,1)S(1)}, bf16[32,6,1,128]{3,2,1,0:T(2,128)(2,1)S(1)}, u32[]{:S(2)}, u32[]{:S(2)}) %collective-permute-start.3) | collective-permute-done | bytes 49184 | tf_op jit(solution)/shard_map/ppermute | solution.py:17
  26.8 3.2 %reshape.229 = bf16[32,6,6,1,8,17]{5,4,2,1,0,3:T(8,128)(2,1)S(1)} reshape(bf16[32,6,6,1,136]{4,2,1,0,3:T(8,128)(2,1)} %pad.45) | data formatting | bytes 626688 | tf_op jit(solution)/shard_map/conv_general_dilated | solution.py:26
  30.0 3.9 %copy.280 = bf16[32,6,6,1,8,17]{0,4,5,2,1,3:T(8,128)(2,1)} copy(bf16[32,6,6,1,8,17]{5,4,2,1,0,3:T(8,128)(2,1)S(1)} %reshape.229) | data formatting | bytes 626688 | tf_op jit(solution)/shard_map/conv_general_dilated | solution.py:26
  34.8 3.4 %fusion.42 = f32[4,4,8,17,32]{4,2,3,1,0:T(8,128)S(1)} fusion(bf16[3,3,3,32,32]{4,3,2,1,0:T(8,128)(2,1)S(1)} %copy-done.8, bf16[32,6,6,1,7,2]{0,4,5,2,1,3:T(8,128)(2,1)S(1)} %slice.152, bf16[32,6,6,1,8,17]{0,4,5,2,1,3:T(8,128)(2,1)} %copy.280, pred[8,17]{0,1:T(8,128)(4,1)S(1)} %copy-done.12), kind=kOutput, calls=%fused_computation.37 | convolution fusion | flops 121444352 | bytes 679560 | tf_op jit(solution)/shard_map/conv_general_dilated | solution.py:26
  39.5 2.1 collective-permute-start.4
  41.5 4.5 %collective-permute-start.5 = (bf16[32,1,2,64]{3,0,2,1:T(8,128)(2,1)S(1)}, bf16[32,1,2,64]{3,0,2,1:T(8,128)(2,1)S(1)}, u32[]{:S(2)}, u32[]{:S(2)}) collective-permute-start(bf16[32,1,2,64]{3,0,2,1:T(8,128)(2,1)S(1)} %get-tuple-element.53), channel_id=1, source_target_pairs={{4,0},{8,4},{12,8},{16,12},{20,16},{24,20},{28,24},{5,1},{9,5},{13... | collective-permute-start | bytes 24584 | tf_op jit(solution)/shard_map/ppermute | solution.py:17
  46.2 1.3 collective-permute-done.5
  47.5 3.5 %collective-permute-start.6 = (bf16[32,4,1,64]{3,0,2,1:T(8,128)(2,1)S(1)}, bf16[32,4,1,64]{3,0,2,1:T(8,128)(2,1)S(1)}, u32[]{:S(2)}, u32[]{:S(2)}) collective-permute-start(bf16[32,4,1,64]{3,0,2,1:T(8,128)(2,1)S(1)} %get-tuple-element.48), channel_id=1, source_target_pairs={{0,1},{1,2},{2,3},{4,5},{5,6},{6,7},{8,9},{9,10},{10,11},{12,13},{... | collective-permute-start | bytes 49160 | tf_op jit(solution)/shard_map/ppermute | solution.py:15
  51.0 1.3 collective-permute-start.7
  52.6 4.2 %collective-permute-done.7 = bf16[32,4,1,64]{3,0,2,1:T(8,128)(2,1)S(1)} collective-permute-done((bf16[32,4,1,64]{3,0,2,1:T(8,128)(2,1)S(1)}, bf16[32,4,1,64]{3,0,2,1:T(8,128)(2,1)S(1)}, u32[]{:S(2)}, u32[]{:S(2)}) %collective-permute-start.7) | collective-permute-done | bytes 16416 | tf_op jit(solution)/shard_map/ppermute | solution.py:17
  58.7 3.1 %collective-permute-start.9 = (bf16[64,1,1,32]{0,3,2,1:T(8,128)(2,1)S(1)}, bf16[64,1,1,32]{0,3,2,1:T(8,128)(2,1)S(1)}, u32[]{:S(2)}, u32[]{:S(2)}) collective-permute-start(bf16[64,1,1,32]{0,3,2,1:T(8,128)(2,1)S(1)} %fusion.174), channel_id=1, source_target_pairs={{4,0},{8,4},{12,8},{16,12},{20,16},{24,20},{28,24},{5,1},{9,5},{13... | collective-permute-start | bytes 12296 | tf_op jit(solution)/shard_map/ppermute | solution.py:17
  61.8 1.9 collective-permute-start.8
  63.9 3.5 %collective-permute-start.22 = (bf16[32,6,1,128]{3,2,1,0:T(2,128)(2,1)S(1)}, bf16[32,6,1,128]{3,2,1,0:T(2,128)(2,1)S(1)}, u32[]{:S(2)}, u32[]{:S(2)}) collective-permute-start(bf16[32,6,1,128]{3,2,1,0:T(2,128)(2,1)S(1)} %get-tuple-element.22), channel_id=1, source_target_pairs={{0,1},{1,2},{2,3},{4,5},{5,6},{6,7},{8,9},{9,10},{10,11},{12,13},{... | collective-permute-start | bytes 147464 | tf_op jit(solution)/shard_map/ppermute | solution.py:15
  67.4 1.3 collective-permute-start.23
  68.7 1.3 collective-permute-start.11
  70.0 5.4 %collective-permute-start.10 = (bf16[64,3,1,32]{0,3,2,1:T(8,128)(2,1)S(1)}, bf16[64,3,1,32]{0,3,2,1:T(8,128)(2,1)S(1)}, u32[]{:S(2)}, u32[]{:S(2)}) collective-permute-start(bf16[64,3,1,32]{0,3,2,1:T(8,128)(2,1)S(1)} %pad_maximum_fusion.10), channel_id=1, source_target_pairs={{0,1},{1,2},{2,3},{4,5},{5,6},{6,7},{8,9},{9,10},{10,11},{12,13},{... | collective-permute-start | bytes 36872 | tf_op jit(solution)/shard_map/ppermute | solution.py:15
  76.6 3.1 %reshape.230 = bf16[32,6,6,1,8,17]{5,4,2,1,0,3:T(8,128)(2,1)} reshape(bf16[32,6,6,1,136]{4,2,1,0,3:T(8,128)(2,1)S(1)} %pad.55) | data formatting | bytes 626688 | tf_op jit(solution)/shard_map/conv_general_dilated | solution.py:26
  79.7 4.2 %copy.307 = bf16[32,6,6,1,8,17]{0,4,5,2,1,3:T(8,128)(2,1)S(1)} copy(bf16[32,6,6,1,8,17]{5,4,2,1,0,3:T(8,128)(2,1)} %reshape.230) | data formatting | bytes 626688 | tf_op jit(solution)/shard_map/conv_general_dilated | solution.py:26
  85.3 1.9 collective-permute-start.12
  87.2 4.5 %collective-permute-start.13 = (bf16[64,1,2,64]{0,2,3,1:T(2,128)(2,1)S(1)}, bf16[64,1,2,64]{0,2,3,1:T(2,128)(2,1)S(1)}, u32[]{:S(2)}, u32[]{:S(2)}) collective-permute-start(bf16[64,1,2,64]{0,2,3,1:T(2,128)(2,1)S(1)} %get-tuple-element.47), channel_id=1, source_target_pairs={{4,0},{8,4},{12,8},{16,12},{20,16},{24,20},{28,24},{5,1},{9,5},{13... | collective-permute-start | bytes 49160 | tf_op jit(solution)/shard_map/ppermute | solution.py:17
  91.7 2.6 %fusion.45 = bf16[4,4,8,17,32]{4,2,3,1,0:T(8,128)(2,1)S(1)} fusion(bf16[3,3,3,32,32]{4,3,2,1,0:T(8,128)(2,1)} %param.15, bf16[32,6,6,1,7,2]{0,4,5,2,1,3:T(8,128)(2,1)S(1)} %slice.175, bf16[32,6,6,1,8,17]{0,4,5,2,1,3:T(8,128)(2,1)S(1)} %copy.307, pred[8,17]{0,1:T(8,128)(4,1)S(1)} %copy-done.12), kind=kOutput, calls=%fused_computation.38 | convolution fusion | flops 121513984 | bytes 540296 | tf_op jit(solution)/shard_map/conv_general_dilated | solution.py:26
  96.2 3.9 %collective-permute-start.14 = (bf16[64,4,1,64]{0,2,3,1:T(2,128)(2,1)}, bf16[64,4,1,64]{0,2,3,1:T(2,128)(2,1)S(1)}, u32[]{:S(2)}, u32[]{:S(2)}) collective-permute-start(bf16[64,4,1,64]{0,2,3,1:T(2,128)(2,1)} %get-tuple-element.36), channel_id=1, source_target_pairs={{0,1},{1,2},{2,3},{4,5},{5,6},{6,7},{8,9},{9,10},{10,11},{12,13},{... | collective-permute-start | bytes 98312 | tf_op jit(solution)/shard_map/ppermute | solution.py:15
  100.1 1.3 collective-permute-start.15
  102.9 4.4 %collective-permute-done.15 = bf16[64,4,1,64]{0,2,3,1:T(2,128)(2,1)} collective-permute-done((bf16[64,4,1,64]{0,2,3,1:T(2,128)(2,1)}, bf16[64,4,1,64]{0,2,3,1:T(2,128)(2,1)}, u32[]{:S(2)}, u32[]{:S(2)}) %collective-permute-start.15) | collective-permute-done | bytes 32800 | tf_op jit(solution)/shard_map/ppermute | solution.py:17
  107.3 1.5 fusion.105
  110.0 1.9 collective-permute-start.24
  111.9 4.5 %collective-permute-start.25 = (bf16[32,1,2,64]{3,0,2,1:T(8,128)(2,1)S(1)}, bf16[32,1,2,64]{3,0,2,1:T(8,128)(2,1)S(1)}, u32[]{:S(2)}, u32[]{:S(2)}) collective-permute-start(bf16[32,1,2,64]{3,0,2,1:T(8,128)(2,1)S(1)} %get-tuple-element.51), channel_id=1, source_target_pairs={{4,0},{8,4},{12,8},{16,12},{20,16},{24,20},{28,24},{5,1},{9,5},{13... | collective-permute-start | bytes 24584 | tf_op jit(solution)/shard_map/ppermute | solution.py:17
  116.4 1.4 collective-permute-done.25
  117.9 2.2 %collective-permute-start.26 = (bf16[32,4,1,64]{3,0,2,1:T(8,128)(2,1)S(1)}, bf16[32,4,1,64]{3,0,2,1:T(8,128)(2,1)S(1)}, u32[]{:S(2)}, u32[]{:S(2)}) collective-permute-start(bf16[32,4,1,64]{3,0,2,1:T(8,128)(2,1)S(1)} %get-tuple-element.42), channel_id=1, source_target_pairs={{0,1},{1,2},{2,3},{4,5},{5,6},{6,7},{8,9},{9,10},{10,11},{12,13},{... | collective-permute-start | bytes 49160 | tf_op jit(solution)/shard_map/ppermute | solution.py:15
  120.1 1.3 collective-permute-start.27
  121.7 4.2 %collective-permute-done.27 = bf16[32,4,1,64]{3,0,2,1:T(8,128)(2,1)S(1)} collective-permute-done((bf16[32,4,1,64]{3,0,2,1:T(8,128)(2,1)S(1)}, bf16[32,4,1,64]{3,0,2,1:T(8,128)(2,1)S(1)}, u32[]{:S(2)}, u32[]{:S(2)}) %collective-permute-start.27) | collective-permute-done | bytes 16416 | tf_op jit(solution)/shard_map/ppermute | solution.py:17
  127.7 3.1 %collective-permute-start.29 = (bf16[128,1,1,32]{0,3,2,1:T(8,128)(2,1)S(1)}, bf16[128,1,1,32]{0,3,2,1:T(8,128)(2,1)S(1)}, u32[]{:S(2)}, u32[]{:S(2)}) collective-permute-start(bf16[128,1,1,32]{0,3,2,1:T(8,128)(2,1)S(1)} %fusion.60), channel_id=1, source_target_pairs={{4,0},{8,4},{12,8},{16,12},{20,16},{24,20},{28,24},{5,1},{9,5},{13... | collective-permute-start | bytes 24584 | tf_op jit(solution)/shard_map/ppermute | solution.py:17
  130.8 1.9 collective-permute-start.28
  132.8 3.9 %collective-permute-done.28 = bf16[128,1,1,32]{0,3,2,1:T(8,128)(2,1)S(1)} collective-permute-done((bf16[128,1,1,32]{0,3,2,1:T(8,128)(2,1)S(1)}, bf16[128,1,1,32]{0,3,2,1:T(8,128)(2,1)S(1)}, u32[]{:S(2)}, u32[]{:S(2)}) %collective-permute-start.28) | collective-permute-done | bytes 8224 | tf_op jit(solution)/shard_map/ppermute | solution.py:15
  136.7 1.3 collective-permute-start.31
  138.0 4.5 %collective-permute-start.30 = (bf16[128,3,1,32]{0,3,2,1:T(8,128)(2,1)S(1)}, bf16[128,3,1,32]{0,3,2,1:T(8,128)(2,1)S(1)}, u32[]{:S(2)}, u32[]{:S(2)}) collective-permute-start(bf16[128,3,1,32]{0,3,2,1:T(8,128)(2,1)S(1)} %pad_maximum_fusion.11), channel_id=1, source_target_pairs={{0,1},{1,2},{2,3},{4,5},{5,6},{6,7},{8,9},{9,10},{10,11},{12,13},{... | collective-permute-start | bytes 73736 | tf_op jit(solution)/shard_map/ppermute | solution.py:15
  142.6 1.4 collective-permute-done.30
  144.7 1.9 collective-permute-start.32
  146.7 4.5 %collective-permute-start.33 = (bf16[64,1,2,64]{0,2,3,1:T(2,128)(2,1)S(1)}, bf16[64,1,2,64]{0,2,3,1:T(2,128)(2,1)S(1)}, u32[]{:S(2)}, u32[]{:S(2)}) collective-permute-start(bf16[64,1,2,64]{0,2,3,1:T(2,128)(2,1)S(1)} %get-tuple-element.41), channel_id=1, source_target_pairs={{4,0},{8,4},{12,8},{16,12},{20,16},{24,20},{28,24},{5,1},{9,5},{13... | collective-permute-start | bytes 49160 | tf_op jit(solution)/shard_map/ppermute | solution.py:17
  151.2 1.6 collective-permute-done.33
  153.2 4.2 %collective-permute-start.34 = (bf16[64,4,1,64]{0,2,3,1:T(2,128)(2,1)S(1)}, bf16[64,4,1,64]{0,2,3,1:T(2,128)(2,1)S(1)}, u32[]{:S(2)}, u32[]{:S(2)}) collective-permute-start(bf16[64,4,1,64]{0,2,3,1:T(2,128)(2,1)S(1)} %get-tuple-element.30), channel_id=1, source_target_pairs={{0,1},{1,2},{2,3},{4,5},{5,6},{6,7},{8,9},{9,10},{10,11},{12,13},{... | collective-permute-start | bytes 98312 | tf_op jit(solution)/shard_map/ppermute | solution.py:15
  157.5 1.5 collective-permute-start.35
  160.2 4.4 %collective-permute-done.35 = bf16[64,4,1,64]{0,2,3,1:T(2,128)(2,1)S(1)} collective-permute-done((bf16[64,4,1,64]{0,2,3,1:T(2,128)(2,1)S(1)}, bf16[64,4,1,64]{0,2,3,1:T(2,128)(2,1)S(1)}, u32[]{:S(2)}, u32[]{:S(2)}) %collective-permute-start.35) | collective-permute-done | bytes 32800 | tf_op jit(solution)/shard_map/ppermute | solution.py:17
  167.1 1.9 collective-permute-start.36
  169.0 4.5 %collective-permute-start.37 = (bf16[32,1,4,128]{3,0,2,1:T(8,128)(2,1)S(1)}, bf16[32,1,4,128]{3,0,2,1:T(8,128)(2,1)S(1)}, u32[]{:S(2)}, u32[]{:S(2)}) collective-permute-start(bf16[32,1,4,128]{3,0,2,1:T(8,128)(2,1)S(1)} %get-tuple-element.29), channel_id=1, source_target_pairs={{4,0},{8,4},{12,8},{16,12},{20,16},{24,20},{28,24},{5,1},{9,5},{13... | collective-permute-start | bytes 98312 | tf_op jit(solution)/shard_map/ppermute | solution.py:17
  173.5 1.9 collective-permute-start.16
  175.5 4.5 %collective-permute-start.17 = (bf16[32,1,4,128]{3,0,2,1:T(8,128)(2,1)S(1)}, bf16[32,1,4,128]{3,0,2,1:T(8,128)(2,1)S(1)}, u32[]{:S(2)}, u32[]{:S(2)}) collective-permute-start(bf16[32,1,4,128]{3,0,2,1:T(8,128)(2,1)S(1)} %get-tuple-element.35), channel_id=1, source_target_pairs={{4,0},{8,4},{12,8},{16,12},{20,16},{24,20},{28,24},{5,1},{9,5},{13... | collective-permute-start | bytes 98312 | tf_op jit(solution)/shard_map/ppermute | solution.py:17
  180.1 2.2 %collective-permute-start.38 = (bf16[32,6,1,128]{3,0,2,1:T(8,128)(2,1)S(1)}, bf16[32,6,1,128]{3,0,2,1:T(8,128)(2,1)S(1)}, u32[]{:S(2)}, u32[]{:S(2)}) collective-permute-start(bf16[32,6,1,128]{3,0,2,1:T(8,128)(2,1)S(1)} %get-tuple-element.20), channel_id=1, source_target_pairs={{0,1},{1,2},{2,3},{4,5},{5,6},{6,7},{8,9},{9,10},{10,11},{12,13},{... | collective-permute-start | bytes 147464 | tf_op jit(solution)/shard_map/ppermute | solution.py:15
  182.3 1.3 collective-permute-start.39
  183.6 4.5 %collective-permute-start.18 = (bf16[32,6,1,128]{3,0,2,1:T(8,128)(2,1)S(1)}, bf16[32,6,1,128]{3,0,2,1:T(8,128)(2,1)S(1)}, u32[]{:S(2)}, u32[]{:S(2)}) collective-permute-start(bf16[32,6,1,128]{3,0,2,1:T(8,128)(2,1)S(1)} %get-tuple-element.24), channel_id=1, source_target_pairs={{0,1},{1,2},{2,3},{4,5},{5,6},{6,7},{8,9},{9,10},{10,11},{12,13},{... | collective-permute-start | bytes 147464 | tf_op jit(solution)/shard_map/ppermute | solution.py:15
  188.2 1.3 collective-permute-start.19
  190.0 4.2 %collective-permute-done.19 = bf16[32,6,1,128]{3,0,2,1:T(8,128)(2,1)S(1)} collective-permute-done((bf16[32,6,1,128]{3,0,2,1:T(8,128)(2,1)S(1)}, bf16[32,6,1,128]{3,0,2,1:T(8,128)(2,1)S(1)}, u32[]{:S(2)}, u32[]{:S(2)}) %collective-permute-start.19) | collective-permute-done | bytes 49184 | tf_op jit(solution)/shard_map/ppermute | solution.py:17
  195.5 3.0 %reshape.132 = bf16[32,6,6,1,8,17]{5,4,0,2,1,3:T(8,128)(2,1)S(1)} reshape(bf16[32,6,6,1,136]{4,0,2,1,3:T(8,128)(2,1)} %pad.53) | data formatting | bytes 626688 | tf_op jit(solution)/shard_map/conv_general_dilated | solution.py:26
  198.5 3.0 %copy.303 = bf16[32,6,6,1,8,17]{0,4,5,2,1,3:T(8,128)(2,1)} copy(bf16[32,6,6,1,8,17]{5,4,0,2,1,3:T(8,128)(2,1)S(1)} %reshape.132) | data formatting | bytes 626688 | tf_op jit(solution)/shard_map/conv_general_dilated | solution.py:26
  202.5 3.4 %fusion.48 = bf16[4,4,8,17,32]{4,2,3,1,0:T(8,128)(2,1)S(1)} fusion(bf16[3,3,3,32,32]{4,3,2,1,0:T(8,128)(2,1)} %param.15, bf16[32,6,6,1,7,2]{0,4,5,2,1,3:T(8,128)(2,1)S(1)} %slice.171, bf16[32,6,6,1,8,17]{0,4,5,2,1,3:T(8,128)(2,1)} %copy.303, pred[8,17]{0,1:T(8,128)(4,1)S(1)} %copy-done.12), kind=kOutput, calls=%fused_computation.39 | convolution fusion | flops 121513984 | bytes 540296 | tf_op jit(solution)/shard_map/conv_general_dilated | solution.py:26
  207.2 1.7 reshape.169
  209.0 3.0 %copy.327 = bf16[32,6,6,1,8,17]{0,4,5,2,1,3:T(8,128)(2,1)} copy(bf16[32,6,6,1,8,17]{5,4,0,2,1,3:T(8,128)(2,1)S(1)} %reshape.169) | data formatting | bytes 626688 | tf_op jit(solution)/shard_map/conv_general_dilated | solution.py:26
  212.9 3.0 %fusion.51 = bf16[4,4,8,17,32]{4,2,3,1,0:T(8,128)(2,1)S(1)} fusion(bf16[3,3,3,32,32]{4,3,2,1,0:T(8,128)(2,1)S(1)} %copy-done.9, bf16[32,6,6,1,7,2]{0,4,5,2,1,3:T(8,128)(2,1)S(1)} %slice.194, bf16[32,6,6,1,8,17]{0,4,5,2,1,3:T(8,128)(2,1)} %copy.327, pred[8,17]{0,1:T(8,128)(4,1)S(1)} %copy-done.12), kind=kOutput, calls=%fused_computation.40 | convolution fusion | flops 121513984 | bytes 540296 | tf_op jit(solution)/shard_map/conv_general_dilated | solution.py:26
  (191 shorter events, 30.0 us)
Async XLA Ops:
  0.6 83.6 %copy-start = (bf16[3,3,3,64,128]{4,3,2,1,0:T(8,128)(2,1)S(1)}, bf16[3,3,3,64,128]{4,3,2,1,0:T(8,128)(2,1)}, u32[]{:S(2)}) copy-start(bf16[3,3,3,64,128]{4,3,2,1,0:T(8,128)(2,1)} %param.12) | copy-start | bytes 1327108
  1.5 13.0 %collective-permute-start.1 = (bf16[32,1,4,128]{3,2,1,0:T(4,128)(2,1)S(1)}, bf16[32,1,4,128]{3,2,1,0:T(4,128)(2,1)S(1)}, u32[]{:S(2)}, u32[]{:S(2)}) collective-permute-start(bf16[32,1,4,128]{3,2,1,0:T(4,128)(2,1)S(1)} %get-tuple-element.38), channel_id=1, source_target_pairs={{4,0},{8,4},{12,8},{16,12},{20,16},{24,20},{28,24},{5,1},{9,5},{13... | collective-permute-start | bytes 98312 | tf_op jit(solution)/shard_map/ppermute | solution.py:17
  4.3 9.2 %collective-permute-start = (bf16[32,1,4,128]{3,2,1,0:T(4,128)(2,1)S(1)}, bf16[32,1,4,128]{3,2,1,0:T(4,128)(2,1)S(1)}, u32[]{:S(2)}, u32[]{:S(2)}) collective-permute-start(bf16[32,1,4,128]{3,2,1,0:T(4,128)(2,1)S(1)} %get-tuple-element.39), channel_id=1, source_target_pairs={{0,4},{4,8},{8,12},{12,16},{16,20},{20,24},{24,28},{1,5},{5,9},{9,... | collective-permute-start | bytes 98312 | tf_op jit(solution)/shard_map/ppermute | solution.py:15
  7.0 45.3 %collective-permute-start.21 = (bf16[32,1,4,128]{3,2,1,0:T(4,128)(2,1)S(1)}, bf16[32,1,4,128]{3,2,1,0:T(4,128)(2,1)S(1)}, u32[]{:S(2)}, u32[]{:S(2)}) collective-permute-start(bf16[32,1,4,128]{3,2,1,0:T(4,128)(2,1)S(1)} %get-tuple-element.32), channel_id=1, source_target_pairs={{4,0},{8,4},{12,8},{16,12},{20,16},{24,20},{28,24},{5,1},{9,5},{13... | collective-permute-start | bytes 98312 | tf_op jit(solution)/shard_map/ppermute | solution.py:17
  11.6 7.9 %collective-permute-start.20 = (bf16[32,1,4,128]{3,2,1,0:T(4,128)(2,1)S(1)}, bf16[32,1,4,128]{3,2,1,0:T(4,128)(2,1)S(1)}, u32[]{:S(2)}, u32[]{:S(2)}) collective-permute-start(bf16[32,1,4,128]{3,2,1,0:T(4,128)(2,1)S(1)} %get-tuple-element.33), channel_id=1, source_target_pairs={{0,4},{4,8},{8,12},{12,16},{16,20},{20,24},{24,28},{1,5},{5,9},{9,... | collective-permute-start | bytes 98312 | tf_op jit(solution)/shard_map/ppermute | solution.py:15
  14.7 5.7 %collective-permute-start.2 = (bf16[32,6,1,128]{3,2,1,0:T(2,128)(2,1)S(1)}, bf16[32,6,1,128]{3,2,1,0:T(2,128)(2,1)S(1)}, u32[]{:S(2)}, u32[]{:S(2)}) collective-permute-start(bf16[32,6,1,128]{3,2,1,0:T(2,128)(2,1)S(1)} %get-tuple-element.26), channel_id=1, source_target_pairs={{0,1},{1,2},{2,3},{4,5},{5,6},{6,7},{8,9},{9,10},{10,11},{12,13},{... | collective-permute-start | bytes 147464 | tf_op jit(solution)/shard_map/ppermute | solution.py:15
  18.2 6.5 %collective-permute-start.3 = (bf16[32,6,1,128]{3,2,1,0:T(2,128)(2,1)S(1)}, bf16[32,6,1,128]{3,2,1,0:T(2,128)(2,1)S(1)}, u32[]{:S(2)}, u32[]{:S(2)}) collective-permute-start(bf16[32,6,1,128]{3,2,1,0:T(2,128)(2,1)S(1)} %get-tuple-element.27), channel_id=1, source_target_pairs={{1,0},{2,1},{3,2},{5,4},{6,5},{7,6},{9,8},{10,9},{11,10},{13,12},{... | collective-permute-start | bytes 147464 | tf_op jit(solution)/shard_map/ppermute | solution.py:17
  30.0 4.9 %copy-start.8 = (bf16[3,3,3,32,32]{4,3,2,1,0:T(8,128)(2,1)S(1)}, bf16[3,3,3,32,32]{4,3,2,1,0:T(8,128)(2,1)}, u32[]{:S(2)}) copy-start(bf16[3,3,3,32,32]{4,3,2,1,0:T(8,128)(2,1)} %param.10) | copy-start | bytes 165892
  30.0 4.9 %copy-start.12 = (pred[8,17]{0,1:T(8,128)(4,1)S(1)}, pred[8,17]{0,1:T(8,128)(4,1)}, u32[]{:S(2)}) copy-start(pred[8,17]{0,1:T(8,128)(4,1)} %constant.81) | copy-start | bytes 412
  38.8 7.3 %copy-start.1 = (bf16[32,4,4,128]{3,2,1,0:T(4,128)(2,1)S(1)}, bf16[32,4,4,128]{3,2,1,0:T(4,128)(2,1)}, u32[]{:S(2)}) copy-start(bf16[32,4,4,128]{3,2,1,0:T(4,128)(2,1)} %param.9) | copy-start | bytes 393220
  39.4 18.0 %copy-start.6 = (bf16[3,3,3,32,64]{4,3,2,1,0:T(8,128)(2,1)S(1)}, bf16[3,3,3,32,64]{4,3,2,1,0:T(8,128)(2,1)}, u32[]{:S(2)}) copy-start(bf16[3,3,3,32,64]{4,3,2,1,0:T(8,128)(2,1)} %param.11) | copy-start | bytes 331780
  39.4 18.0 %copy-start.13 = (pred[8,9]{0,1:T(8,128)(4,1)S(1)}, pred[8,9]{0,1:T(8,128)(4,1)}, u32[]{:S(2)}) copy-start(pred[8,9]{0,1:T(8,128)(4,1)} %constant.82) | copy-start | bytes 220
  39.5 6.7 %collective-permute-start.4 = (bf16[32,1,2,64]{3,0,2,1:T(8,128)(2,1)S(1)}, bf16[32,1,2,64]{3,0,2,1:T(8,128)(2,1)S(1)}, u32[]{:S(2)}, u32[]{:S(2)}) collective-permute-start(bf16[32,1,2,64]{3,0,2,1:T(8,128)(2,1)S(1)} %get-tuple-element.52), channel_id=1, source_target_pairs={{0,4},{4,8},{8,12},{12,16},{16,20},{20,24},{24,28},{1,5},{5,9},{9,... | collective-permute-start | bytes 24584 | tf_op jit(solution)/shard_map/ppermute | solution.py:15
  41.5 6.0 %collective-permute-start.5 = (bf16[32,1,2,64]{3,0,2,1:T(8,128)(2,1)S(1)}, bf16[32,1,2,64]{3,0,2,1:T(8,128)(2,1)S(1)}, u32[]{:S(2)}, u32[]{:S(2)}) collective-permute-start(bf16[32,1,2,64]{3,0,2,1:T(8,128)(2,1)S(1)} %get-tuple-element.53), channel_id=1, source_target_pairs={{4,0},{8,4},{12,8},{16,12},{20,16},{24,20},{28,24},{5,1},{9,5},{13... | collective-permute-start | bytes 24584 | tf_op jit(solution)/shard_map/ppermute | solution.py:17
  47.5 5.1 %collective-permute-start.6 = (bf16[32,4,1,64]{3,0,2,1:T(8,128)(2,1)S(1)}, bf16[32,4,1,64]{3,0,2,1:T(8,128)(2,1)S(1)}, u32[]{:S(2)}, u32[]{:S(2)}) collective-permute-start(bf16[32,4,1,64]{3,0,2,1:T(8,128)(2,1)S(1)} %get-tuple-element.48), channel_id=1, source_target_pairs={{0,1},{1,2},{2,3},{4,5},{5,6},{6,7},{8,9},{9,10},{10,11},{12,13},{... | collective-permute-start | bytes 49160 | tf_op jit(solution)/shard_map/ppermute | solution.py:15
  51.0 5.8 %collective-permute-start.7 = (bf16[32,4,1,64]{3,0,2,1:T(8,128)(2,1)S(1)}, bf16[32,4,1,64]{3,0,2,1:T(8,128)(2,1)S(1)}, u32[]{:S(2)}, u32[]{:S(2)}) collective-permute-start(bf16[32,4,1,64]{3,0,2,1:T(8,128)(2,1)S(1)} %get-tuple-element.49), channel_id=1, source_target_pairs={{1,0},{2,1},{3,2},{5,4},{6,5},{7,6},{9,8},{10,9},{11,10},{13,12},{... | collective-permute-start | bytes 49160 | tf_op jit(solution)/shard_map/ppermute | solution.py:17
  58.7 10.0 %collective-permute-start.9 = (bf16[64,1,1,32]{0,3,2,1:T(8,128)(2,1)S(1)}, bf16[64,1,1,32]{0,3,2,1:T(8,128)(2,1)S(1)}, u32[]{:S(2)}, u32[]{:S(2)}) collective-permute-start(bf16[64,1,1,32]{0,3,2,1:T(8,128)(2,1)S(1)} %fusion.174), channel_id=1, source_target_pairs={{4,0},{8,4},{12,8},{16,12},{20,16},{24,20},{28,24},{5,1},{9,5},{13... | collective-permute-start | bytes 12296 | tf_op jit(solution)/shard_map/ppermute | solution.py:17
  61.8 6.9 %collective-permute-start.8 = (bf16[64,1,1,32]{0,3,2,1:T(8,128)(2,1)S(1)}, bf16[64,1,1,32]{0,3,2,1:T(8,128)(2,1)S(1)}, u32[]{:S(2)}, u32[]{:S(2)}) collective-permute-start(bf16[64,1,1,32]{0,3,2,1:T(8,128)(2,1)S(1)} %fusion.174), channel_id=1, source_target_pairs={{0,4},{4,8},{8,12},{12,16},{16,20},{20,24},{24,28},{1,5},{5,9},{9,... | collective-permute-start | bytes 12296 | tf_op jit(solution)/shard_map/ppermute | solution.py:15
  63.9 11.5 %collective-permute-start.22 = (bf16[32,6,1,128]{3,2,1,0:T(2,128)(2,1)S(1)}, bf16[32,6,1,128]{3,2,1,0:T(2,128)(2,1)S(1)}, u32[]{:S(2)}, u32[]{:S(2)}) collective-permute-start(bf16[32,6,1,128]{3,2,1,0:T(2,128)(2,1)S(1)} %get-tuple-element.22), channel_id=1, source_target_pairs={{0,1},{1,2},{2,3},{4,5},{5,6},{6,7},{8,9},{9,10},{10,11},{12,13},{... | collective-permute-start | bytes 147464 | tf_op jit(solution)/shard_map/ppermute | solution.py:15
  67.4 8.0 %collective-permute-start.23 = (bf16[32,6,1,128]{3,2,1,0:T(2,128)(2,1)S(1)}, bf16[32,6,1,128]{3,2,1,0:T(2,128)(2,1)S(1)}, u32[]{:S(2)}, u32[]{:S(2)}) collective-permute-start(bf16[32,6,1,128]{3,2,1,0:T(2,128)(2,1)S(1)} %get-tuple-element.23), channel_id=1, source_target_pairs={{1,0},{2,1},{3,2},{5,4},{6,5},{7,6},{9,8},{10,9},{11,10},{13,12},{... | collective-permute-start | bytes 147464 | tf_op jit(solution)/shard_map/ppermute | solution.py:17
  68.7 15.3 %collective-permute-start.11 = (bf16[64,3,1,32]{0,3,2,1:T(8,128)(2,1)S(1)}, bf16[64,3,1,32]{0,3,2,1:T(8,128)(2,1)S(1)}, u32[]{:S(2)}, u32[]{:S(2)}) collective-permute-start(bf16[64,3,1,32]{0,3,2,1:T(8,128)(2,1)S(1)} %pad_maximum_fusion.10), channel_id=1, source_target_pairs={{1,0},{2,1},{3,2},{5,4},{6,5},{7,6},{9,8},{10,9},{11,10},{13,12},{... | collective-permute-start | bytes 36872 | tf_op jit(solution)/shard_map/ppermute | solution.py:17
  70.0 14.1 %collective-permute-start.10 = (bf16[64,3,1,32]{0,3,2,1:T(8,128)(2,1)S(1)}, bf16[64,3,1,32]{0,3,2,1:T(8,128)(2,1)S(1)}, u32[]{:S(2)}, u32[]{:S(2)}) collective-permute-start(bf16[64,3,1,32]{0,3,2,1:T(8,128)(2,1)S(1)} %pad_maximum_fusion.10), channel_id=1, source_target_pairs={{0,1},{1,2},{2,3},{4,5},{5,6},{6,7},{8,9},{9,10},{10,11},{12,13},{... | collective-permute-start | bytes 36872 | tf_op jit(solution)/shard_map/ppermute | solution.py:15
  83.9 0.7 copy-start.15
  83.9 1.0 copy-start.10
  85.3 9.8 %collective-permute-start.12 = (bf16[64,1,2,64]{0,2,3,1:T(2,128)(2,1)S(1)}, bf16[64,1,2,64]{0,2,3,1:T(2,128)(2,1)S(1)}, u32[]{:S(2)}, u32[]{:S(2)}) collective-permute-start(bf16[64,1,2,64]{0,2,3,1:T(2,128)(2,1)S(1)} %get-tuple-element.46), channel_id=1, source_target_pairs={{0,4},{4,8},{8,12},{12,16},{16,20},{20,24},{24,28},{1,5},{5,9},{9,... | collective-permute-start | bytes 49160 | tf_op jit(solution)/shard_map/ppermute | solution.py:15
  87.2 7.9 %collective-permute-start.13 = (bf16[64,1,2,64]{0,2,3,1:T(2,128)(2,1)S(1)}, bf16[64,1,2,64]{0,2,3,1:T(2,128)(2,1)S(1)}, u32[]{:S(2)}, u32[]{:S(2)}) collective-permute-start(bf16[64,1,2,64]{0,2,3,1:T(2,128)(2,1)S(1)} %get-tuple-element.47), channel_id=1, source_target_pairs={{4,0},{8,4},{12,8},{16,12},{20,16},{24,20},{28,24},{5,1},{9,5},{13... | collective-permute-start | bytes 49160 | tf_op jit(solution)/shard_map/ppermute | solution.py:17
  95.0 5.1 %copy-start.2 = (bf16[64,1,2,64]{0,2,3,1:T(2,128)(2,1)}, bf16[64,1,2,64]{0,2,3,1:T(2,128)(2,1)S(1)}, u32[]{:S(2)}) copy-start(bf16[64,1,2,64]{0,2,3,1:T(2,128)(2,1)S(1)} %collective-permute-done.13) | copy-start | bytes 49156
  96.2 6.7 %collective-permute-start.14 = (bf16[64,4,1,64]{0,2,3,1:T(2,128)(2,1)}, bf16[64,4,1,64]{0,2,3,1:T(2,128)(2,1)S(1)}, u32[]{:S(2)}, u32[]{:S(2)}) collective-permute-start(bf16[64,4,1,64]{0,2,3,1:T(2,128)(2,1)} %get-tuple-element.36), channel_id=1, source_target_pairs={{0,1},{1,2},{2,3},{4,5},{5,6},{6,7},{8,9},{9,10},{10,11},{12,13},{... | collective-permute-start | bytes 98312 | tf_op jit(solution)/shard_map/ppermute | solution.py:15
  100.1 7.2 %collective-permute-start.15 = (bf16[64,4,1,64]{0,2,3,1:T(2,128)(2,1)}, bf16[64,4,1,64]{0,2,3,1:T(2,128)(2,1)}, u32[]{:S(2)}, u32[]{:S(2)}) collective-permute-start(bf16[64,4,1,64]{0,2,3,1:T(2,128)(2,1)} %get-tuple-element.37), channel_id=1, source_target_pairs={{1,0},{2,1},{3,2},{5,4},{6,5},{7,6},{9,8},{10,9},{11,10},{13,12},{... | collective-permute-start | bytes 98312 | tf_op jit(solution)/shard_map/ppermute | solution.py:17
  101.5 5.9 %copy-start.3 = (bf16[64,1,2,64]{0,2,3,1:T(2,128)(2,1)S(1)}, bf16[64,1,2,64]{0,2,3,1:T(2,128)(2,1)}, u32[]{:S(2)}) copy-start(bf16[64,1,2,64]{0,2,3,1:T(2,128)(2,1)} %copy-done.2) | copy-start | bytes 49156
  101.8 7.2 %copy-start.14 = (pred[8,9]{0,1:T(8,128)(4,1)S(1)}, pred[8,9]{0,1:T(8,128)(4,1)}, u32[]{:S(2)}) copy-start(pred[8,9]{0,1:T(8,128)(4,1)} %constant.82) | copy-start | bytes 220
  102.6 6.4 %copy-start.4 = (bf16[3,3,3,64,32]{3,4,2,1,0:T(8,128)(2,1)S(1)}, bf16[3,3,3,64,32]{3,4,2,1,0:T(8,128)(2,1)}, u32[]{:S(2)}) copy-start(bf16[3,3,3,64,32]{3,4,2,1,0:T(8,128)(2,1)} %param.14) | copy-start | bytes 331780
  109.8 16.7 %copy-start.5 = (bf16[3,3,3,64,32]{3,4,2,1,0:T(8,128)(2,1)S(1)}, bf16[3,3,3,64,32]{3,4,2,1,0:T(8,128)(2,1)}, u32[]{:S(2)}) copy-start(bf16[3,3,3,64,32]{3,4,2,1,0:T(8,128)(2,1)} %param.14) | copy-start | bytes 331780
  110.0 6.5 %collective-permute-start.24 = (bf16[32,1,2,64]{3,0,2,1:T(8,128)(2,1)S(1)}, bf16[32,1,2,64]{3,0,2,1:T(8,128)(2,1)S(1)}, u32[]{:S(2)}, u32[]{:S(2)}) collective-permute-start(bf16[32,1,2,64]{3,0,2,1:T(8,128)(2,1)S(1)} %get-tuple-element.50), channel_id=1, source_target_pairs={{0,4},{4,8},{8,12},{12,16},{16,20},{20,24},{24,28},{1,5},{5,9},{9,... | collective-permute-start | bytes 24584 | tf_op jit(solution)/shard_map/ppermute | solution.py:15
  111.9 6.0 %collective-permute-start.25 = (bf16[32,1,2,64]{3,0,2,1:T(8,128)(2,1)S(1)}, bf16[32,1,2,64]{3,0,2,1:T(8,128)(2,1)S(1)}, u32[]{:S(2)}, u32[]{:S(2)}) collective-permute-start(bf16[32,1,2,64]{3,0,2,1:T(8,128)(2,1)S(1)} %get-tuple-element.51), channel_id=1, source_target_pairs={{4,0},{8,4},{12,8},{16,12},{20,16},{24,20},{28,24},{5,1},{9,5},{13... | collective-permute-start | bytes 24584 | tf_op jit(solution)/shard_map/ppermute | solution.py:17
  117.9 3.8 %collective-permute-start.26 = (bf16[32,4,1,64]{3,0,2,1:T(8,128)(2,1)S(1)}, bf16[32,4,1,64]{3,0,2,1:T(8,128)(2,1)S(1)}, u32[]{:S(2)}, u32[]{:S(2)}) collective-permute-start(bf16[32,4,1,64]{3,0,2,1:T(8,128)(2,1)S(1)} %get-tuple-element.42), channel_id=1, source_target_pairs={{0,1},{1,2},{2,3},{4,5},{5,6},{6,7},{8,9},{9,10},{10,11},{12,13},{... | collective-permute-start | bytes 49160 | tf_op jit(solution)/shard_map/ppermute | solution.py:15
  120.1 5.8 %collective-permute-start.27 = (bf16[32,4,1,64]{3,0,2,1:T(8,128)(2,1)S(1)}, bf16[32,4,1,64]{3,0,2,1:T(8,128)(2,1)S(1)}, u32[]{:S(2)}, u32[]{:S(2)}) collective-permute-start(bf16[32,4,1,64]{3,0,2,1:T(8,128)(2,1)S(1)} %get-tuple-element.43), channel_id=1, source_target_pairs={{1,0},{2,1},{3,2},{5,4},{6,5},{7,6},{9,8},{10,9},{11,10},{13,12},{... | collective-permute-start | bytes 49160 | tf_op jit(solution)/shard_map/ppermute | solution.py:17
  126.5 1.1 copy-start.11
  126.5 17.7 %copy-start.16 = (pred[8,5]{0,1:T(8,128)(4,1)S(1)}, pred[8,5]{0,1:T(8,128)(4,1)}, u32[]{:S(2)}) copy-start(pred[8,5]{0,1:T(8,128)(4,1)} %constant.83) | copy-start | bytes 124
  127.7 5.0 %collective-permute-start.29 = (bf16[128,1,1,32]{0,3,2,1:T(8,128)(2,1)S(1)}, bf16[128,1,1,32]{0,3,2,1:T(8,128)(2,1)S(1)}, u32[]{:S(2)}, u32[]{:S(2)}) collective-permute-start(bf16[128,1,1,32]{0,3,2,1:T(8,128)(2,1)S(1)} %fusion.60), channel_id=1, source_target_pairs={{4,0},{8,4},{12,8},{16,12},{20,16},{24,20},{28,24},{5,1},{9,5},{13... | collective-permute-start | bytes 24584 | tf_op jit(solution)/shard_map/ppermute | solution.py:17
  130.8 5.9 %collective-permute-start.28 = (bf16[128,1,1,32]{0,3,2,1:T(8,128)(2,1)S(1)}, bf16[128,1,1,32]{0,3,2,1:T(8,128)(2,1)S(1)}, u32[]{:S(2)}, u32[]{:S(2)}) collective-permute-start(bf16[128,1,1,32]{0,3,2,1:T(8,128)(2,1)S(1)} %fusion.60), channel_id=1, source_target_pairs={{0,4},{4,8},{8,12},{12,16},{16,20},{20,24},{24,28},{1,5},{5,9},{9,... | collective-permute-start | bytes 24584 | tf_op jit(solution)/shard_map/ppermute | solution.py:15
  136.7 5.9 %collective-permute-start.31 = (bf16[128,3,1,32]{0,3,2,1:T(8,128)(2,1)S(1)}, bf16[128,3,1,32]{0,3,2,1:T(8,128)(2,1)S(1)}, u32[]{:S(2)}, u32[]{:S(2)}) collective-permute-start(bf16[128,3,1,32]{0,3,2,1:T(8,128)(2,1)S(1)} %pad_maximum_fusion.11), channel_id=1, source_target_pairs={{1,0},{2,1},{3,2},{5,4},{6,5},{7,6},{9,8},{10,9},{11,10},{13,12},{... | collective-permute-start | bytes 73736 | tf_op jit(solution)/shard_map/ppermute | solution.py:17
  138.0 6.1 %collective-permute-start.30 = (bf16[128,3,1,32]{0,3,2,1:T(8,128)(2,1)S(1)}, bf16[128,3,1,32]{0,3,2,1:T(8,128)(2,1)S(1)}, u32[]{:S(2)}, u32[]{:S(2)}) collective-permute-start(bf16[128,3,1,32]{0,3,2,1:T(8,128)(2,1)S(1)} %pad_maximum_fusion.11), channel_id=1, source_target_pairs={{0,1},{1,2},{2,3},{4,5},{5,6},{6,7},{8,9},{9,10},{10,11},{12,13},{... | collective-permute-start | bytes 73736 | tf_op jit(solution)/shard_map/ppermute | solution.py:15
  144.7 6.5 %collective-permute-start.32 = (bf16[64,1,2,64]{0,2,3,1:T(2,128)(2,1)S(1)}, bf16[64,1,2,64]{0,2,3,1:T(2,128)(2,1)S(1)}, u32[]{:S(2)}, u32[]{:S(2)}) collective-permute-start(bf16[64,1,2,64]{0,2,3,1:T(2,128)(2,1)S(1)} %get-tuple-element.40), channel_id=1, source_target_pairs={{0,4},{4,8},{8,12},{12,16},{16,20},{20,24},{24,28},{1,5},{5,9},{9,... | collective-permute-start | bytes 49160 | tf_op jit(solution)/shard_map/ppermute | solution.py:15
  146.7 6.1 %collective-permute-start.33 = (bf16[64,1,2,64]{0,2,3,1:T(2,128)(2,1)S(1)}, bf16[64,1,2,64]{0,2,3,1:T(2,128)(2,1)S(1)}, u32[]{:S(2)}, u32[]{:S(2)}) collective-permute-start(bf16[64,1,2,64]{0,2,3,1:T(2,128)(2,1)S(1)} %get-tuple-element.41), channel_id=1, source_target_pairs={{4,0},{8,4},{12,8},{16,12},{20,16},{24,20},{28,24},{5,1},{9,5},{13... | collective-permute-start | bytes 49160 | tf_op jit(solution)/shard_map/ppermute | solution.py:17
  153.2 6.9 %collective-permute-start.34 = (bf16[64,4,1,64]{0,2,3,1:T(2,128)(2,1)S(1)}, bf16[64,4,1,64]{0,2,3,1:T(2,128)(2,1)S(1)}, u32[]{:S(2)}, u32[]{:S(2)}) collective-permute-start(bf16[64,4,1,64]{0,2,3,1:T(2,128)(2,1)S(1)} %get-tuple-element.30), channel_id=1, source_target_pairs={{0,1},{1,2},{2,3},{4,5},{5,6},{6,7},{8,9},{9,10},{10,11},{12,13},{... | collective-permute-start | bytes 98312 | tf_op jit(solution)/shard_map/ppermute | solution.py:15
  157.5 7.1 %collective-permute-start.35 = (bf16[64,4,1,64]{0,2,3,1:T(2,128)(2,1)S(1)}, bf16[64,4,1,64]{0,2,3,1:T(2,128)(2,1)S(1)}, u32[]{:S(2)}, u32[]{:S(2)}) collective-permute-start(bf16[64,4,1,64]{0,2,3,1:T(2,128)(2,1)S(1)} %get-tuple-element.31), channel_id=1, source_target_pairs={{1,0},{2,1},{3,2},{5,4},{6,5},{7,6},{9,8},{10,9},{11,10},{13,12},{... | collective-permute-start | bytes 98312 | tf_op jit(solution)/shard_map/ppermute | solution.py:17
  159.9 5.5 %copy-start.7 = (bf16[3,3,3,32,64]{4,3,2,1,0:T(8,128)(2,1)S(1)}, bf16[3,3,3,32,64]{4,3,2,1,0:T(8,128)(2,1)}, u32[]{:S(2)}) copy-start(bf16[3,3,3,32,64]{4,3,2,1,0:T(8,128)(2,1)} %param.11) | copy-start | bytes 331780
  167.1 13.0 %collective-permute-start.36 = (bf16[32,1,4,128]{3,0,2,1:T(8,128)(2,1)S(1)}, bf16[32,1,4,128]{3,0,2,1:T(8,128)(2,1)S(1)}, u32[]{:S(2)}, u32[]{:S(2)}) collective-permute-start(bf16[32,1,4,128]{3,0,2,1:T(8,128)(2,1)S(1)} %get-tuple-element.28), channel_id=1, source_target_pairs={{0,4},{4,8},{8,12},{12,16},{16,20},{20,24},{24,28},{1,5},{5,9},{9,... | collective-permute-start | bytes 98312 | tf_op jit(solution)/shard_map/ppermute | solution.py:15
  169.0 11.1 %collective-permute-start.37 = (bf16[32,1,4,128]{3,0,2,1:T(8,128)(2,1)S(1)}, bf16[32,1,4,128]{3,0,2,1:T(8,128)(2,1)S(1)}, u32[]{:S(2)}, u32[]{:S(2)}) collective-permute-start(bf16[32,1,4,128]{3,0,2,1:T(8,128)(2,1)S(1)} %get-tuple-element.29), channel_id=1, source_target_pairs={{4,0},{8,4},{12,8},{16,12},{20,16},{24,20},{28,24},{5,1},{9,5},{13... | collective-permute-start | bytes 98312 | tf_op jit(solution)/shard_map/ppermute | solution.py:17
  173.5 10.0 %collective-permute-start.16 = (bf16[32,1,4,128]{3,0,2,1:T(8,128)(2,1)S(1)}, bf16[32,1,4,128]{3,0,2,1:T(8,128)(2,1)S(1)}, u32[]{:S(2)}, u32[]{:S(2)}) collective-permute-start(bf16[32,1,4,128]{3,0,2,1:T(8,128)(2,1)S(1)} %get-tuple-element.34), channel_id=1, source_target_pairs={{0,4},{4,8},{8,12},{12,16},{16,20},{20,24},{24,28},{1,5},{5,9},{9,... | collective-permute-start | bytes 98312 | tf_op jit(solution)/shard_map/ppermute | solution.py:15
  175.5 8.1 %collective-permute-start.17 = (bf16[32,1,4,128]{3,0,2,1:T(8,128)(2,1)S(1)}, bf16[32,1,4,128]{3,0,2,1:T(8,128)(2,1)S(1)}, u32[]{:S(2)}, u32[]{:S(2)}) collective-permute-start(bf16[32,1,4,128]{3,0,2,1:T(8,128)(2,1)S(1)} %get-tuple-element.35), channel_id=1, source_target_pairs={{4,0},{8,4},{12,8},{16,12},{20,16},{24,20},{28,24},{5,1},{9,5},{13... | collective-permute-start | bytes 98312 | tf_op jit(solution)/shard_map/ppermute | solution.py:17
  180.1 9.4 %collective-permute-start.38 = (bf16[32,6,1,128]{3,0,2,1:T(8,128)(2,1)S(1)}, bf16[32,6,1,128]{3,0,2,1:T(8,128)(2,1)S(1)}, u32[]{:S(2)}, u32[]{:S(2)}) collective-permute-start(bf16[32,6,1,128]{3,0,2,1:T(8,128)(2,1)S(1)} %get-tuple-element.20), channel_id=1, source_target_pairs={{0,1},{1,2},{2,3},{4,5},{5,6},{6,7},{8,9},{9,10},{10,11},{12,13},{... | collective-permute-start | bytes 147464 | tf_op jit(solution)/shard_map/ppermute | solution.py:15
  182.3 7.2 %collective-permute-start.39 = (bf16[32,6,1,128]{3,0,2,1:T(8,128)(2,1)S(1)}, bf16[32,6,1,128]{3,0,2,1:T(8,128)(2,1)S(1)}, u32[]{:S(2)}, u32[]{:S(2)}) collective-permute-start(bf16[32,6,1,128]{3,0,2,1:T(8,128)(2,1)S(1)} %get-tuple-element.21), channel_id=1, source_target_pairs={{1,0},{2,1},{3,2},{5,4},{6,5},{7,6},{9,8},{10,9},{11,10},{13,12},{... | collective-permute-start | bytes 147464 | tf_op jit(solution)/shard_map/ppermute | solution.py:17
  183.6 6.3 %collective-permute-start.18 = (bf16[32,6,1,128]{3,0,2,1:T(8,128)(2,1)S(1)}, bf16[32,6,1,128]{3,0,2,1:T(8,128)(2,1)S(1)}, u32[]{:S(2)}, u32[]{:S(2)}) collective-permute-start(bf16[32,6,1,128]{3,0,2,1:T(8,128)(2,1)S(1)} %get-tuple-element.24), channel_id=1, source_target_pairs={{0,1},{1,2},{2,3},{4,5},{5,6},{6,7},{8,9},{9,10},{10,11},{12,13},{... | collective-permute-start | bytes 147464 | tf_op jit(solution)/shard_map/ppermute | solution.py:15
  188.2 6.0 %collective-permute-start.19 = (bf16[32,6,1,128]{3,0,2,1:T(8,128)(2,1)S(1)}, bf16[32,6,1,128]{3,0,2,1:T(8,128)(2,1)S(1)}, u32[]{:S(2)}, u32[]{:S(2)}) collective-permute-start(bf16[32,6,1,128]{3,0,2,1:T(8,128)(2,1)S(1)} %get-tuple-element.25), channel_id=1, source_target_pairs={{1,0},{2,1},{3,2},{5,4},{6,5},{7,6},{9,8},{10,9},{11,10},{13,12},{... | collective-permute-start | bytes 147464 | tf_op jit(solution)/shard_map/ppermute | solution.py:17
  209.0 4.0 %copy-start.9 = (bf16[3,3,3,32,32]{4,3,2,1,0:T(8,128)(2,1)S(1)}, bf16[3,3,3,32,32]{4,3,2,1,0:T(8,128)(2,1)}, u32[]{:S(2)}) copy-start(bf16[3,3,3,32,32]{4,3,2,1,0:T(8,128)(2,1)} %param.10) | copy-start | bytes 165892
where the time goes:
time: 219 us; the launch traced here: 217 us
  starting transfers between devices  111 us (51%)
  local copies, waits for them, and re-layouts  43.6 us (20%)
  waiting for transfers between devices  37.2 us (17%)
  matrix products  16.4 us (7%)
  other arithmetic  7.22 us (3%)
  between operations  2.25 us (1%)
    ppermute x20, starting transfers between devices, extended(): lax.ppermute(tail, axis, [(i, (i + 1) % count) for i in range(ends)])  56.8 us
    ppermute x20, starting transfers between devices, extended(): lax.ppermute(head, axis, [((i + 1) % count, i) for i in range(ends)])  53.9 us
    ppermute x20, waiting for transfers between devices, extended(): lax.ppermute(head, axis, [((i + 1) % count, i) for i in range(ends)])  30 us
    conv_general_dilated x33, local copies, waits for them, and re-layouts, conv_valid(): lax.conv_general_dilated(padded[None], kernel, (1, 1, 1), 'VALID', dimens...  29 us
    conv_general_dilated x10, matrix products, conv_valid(): lax.conv_general_dilated(padded[None], kernel, (1, 1, 1), 'VALID', dimens...  16.1 us
    ppermute x20, waiting for transfers between devices, extended(): lax.ppermute(tail, axis, [(i, (i + 1) % count) for i in range(ends)])  7.11 us
    broadcast_in_dim x10, other arithmetic, conv_valid(): padded[None]  5.02 us
    unnamed x45, local copies, waits for them, and re-layouts  4.39 us
  transfers between devices with their start and end apart: 40, of which 15 were waited for; matrix products, arithmetic and copies ran while one was open for 14% of the time, Pallas kernels for 0%

commit v1 on v0

v1 whole, which is shorter than its diff:
```python
import functools

import jax
import jax.numpy as jnp
from jax import lax
from jax.experimental import pallas as pl
from jax.experimental.pallas import tpu as pltpu
from jax.sharding import PartitionSpec as P

BF = jnp.bfloat16
F32 = jnp.float32
SIDES = tuple((dx, dy) for dx in (-1, 0, 1) for dy in (-1, 0, 1) if (dx, dy) != (0, 0))


def sigmoid(value):
    return jax.nn.sigmoid(value)


def silu(value):
    return value * sigmoid(value)


def slope(value):
    sigma = sigmoid(value)
    return sigma * (1.0 + value * (1.0 - sigma))


def lane_of(value):
    return lax.broadcasted_iota(jnp.int32, value.shape, value.ndim - 1)


def conv(weights, edged, xs, step):
    lanes = edged.shape[2]
    depth = 3 * edged.shape[1]
    rows = weights.shape[0] // 3
    matrix = weights[...]
    outs = []
    for x in range(xs):
        part = jnp.dot(
            matrix, edged[x : x + 3].reshape(depth, lanes), preferred_element_type=F32
        )
        low, mid, high = part[:rows], part[rows : 2 * rows], part[2 * rows :]
        lane = lane_of(low)
        low = jnp.where(lane < step, 0.0, pltpu.roll(low, step, 1))
        high = jnp.where(lane >= lanes - step, 0.0, pltpu.roll(high, lanes - step, 1))
        outs.append(low + mid + high)
    return outs


def block_sum(fields, chans, step):
    outs = []
    for x in range(0, len(fields), 2):
        both = fields[x] + fields[x + 1]
        rows, lanes = both.shape
        both = jnp.concatenate(
            [
                both[y * chans : (y + 1) * chans] + both[(y + 1) * chans : (y + 2) * chans]
                for y in range(0, rows // chans, 2)
            ],
            axis=0,
        )
        lane = lane_of(both)
        other = jnp.where(
            lax.rem(lane // step, 2) == 0,
            pltpu.roll(both, lanes - step, 1),
            pltpu.roll(both, step, 1),
        )
        outs.append(both + other)
    return outs


def spread(fields, chans):
    outs = []
    for field in fields:
        parts = []
        for y in range(field.shape[0] // chans):
            cell = field[y * chans : (y + 1) * chans]
            parts += [cell, cell]
        wide = jnp.concatenate(parts, axis=0)
        outs += [wide, wide]
    return outs


def body(
    wide_count, narrow_count, xs, ys, chans,
    vol, cot, w_first, w_second, w_bottom, lift, lift_t, w_decode, w_final,
    b_first, b_second, b_bottom, b_decode, b_final,
    features_ref, grad_ref,
    e_vol, e_cot, e_p1, e_p2, e_j2, e_j1, e_gd, e_gb, e_gs, e_gf,
    pre_first, hidden_first, grad_joined, pre_second, hidden_second,
    send_sem, recv_sem,
):
    c1, c2, c3 = chans
    x2, y2 = xs // 2, ys // 2
    x3, y3 = x2 // 2, y2 // 2
    me_wide = lax.axis_index("wide")
    me_narrow = lax.axis_index("narrow")

    def exists(dx, dy):
        near_x, near_y = me_wide + dx, me_narrow + dy
        return (
            (near_x >= 0) & (near_x < wide_count) & (near_y >= 0) & (near_y < narrow_count)
        )

    def span(delta, count, sending):
        if delta == 0:
            return 1, count
        if sending:
            return (count if delta > 0 else 1), 1
        return (0 if delta > 0 else count + 1), 1

    def copy_of(index, edged, side, nx, ny, width):
        dx, dy = SIDES[side]

        def part(sending):
            x_at, x_len = span(dx, nx, sending)
            y_at, y_len = span(dy, ny, sending)
            return edged.at[pl.ds(x_at, x_len), pl.ds(y_at * width, y_len * width), :]

        return pltpu.make_async_remote_copy(
            src_ref=part(True),
            dst_ref=part(False),
            send_sem=send_sem.at[index, side],
            recv_sem=recv_sem.at[index, side],
            device_id=(me_wide + dx, me_narrow + dy),
            device_id_type=pl.DeviceIdType.MESH,
        )

    started = []

    def send(index, edged, nx, ny, width):
        for side, (dx, dy) in enumerate(SIDES):
            copy = copy_of(index, edged, side, nx, ny, width)
            pl.when(exists(dx, dy))(copy.start)
        started.append((index, edged, nx, ny, width))

    def receive(index, edged, nx, ny, width):
        for side, (dx, dy) in enumerate(SIDES):
            copy = copy_of(index, edged, side, nx, ny, width)
            pl.when(exists(-dx, -dy))(copy.wait_recv)

    def put(edged, fields, width):
        rows = fields[0].shape[0]
        for x, field in enumerate(fields):
            edged[x + 1, width : width + rows, :] = field.astype(BF)

    def clear(edged, nx, ny, width):
        lanes = edged.shape[2]
        edged[0] = jnp.zeros(((ny + 2) * width, lanes), BF)
        edged[nx + 1] = jnp.zeros(((ny + 2) * width, lanes), BF)
        for x in range(1, nx + 1):
            edged[x, 0:width, :] = jnp.zeros((width, lanes), BF)
            edged[x, (ny + 1) * width : (ny + 2) * width, :] = jnp.zeros((width, lanes), BF)

    spec_vol = (0, e_vol, xs, ys, c1)
    spec_cot = (1, e_cot, xs, ys, c1)
    spec_p1 = (2, e_p1, x2, y2, c1)
    spec_p2 = (3, e_p2, x3, y3, c2)
    spec_j2 = (4, e_j2, x2, y2, c2)
    spec_j1 = (5, e_j1, xs, ys, c1)
    spec_gd = (6, e_gd, x2, y2, c1)
    spec_gb = (7, e_gb, x3, y3, c3)
    spec_gs = (8, e_gs, x2, y2, c2)
    spec_gf = (9, e_gf, xs, ys, c1)
    for spec in (
        spec_vol, spec_cot, spec_p1, spec_p2, spec_j2, spec_j1, spec_gd, spec_gb, spec_gs, spec_gf
    ):
        clear(*spec[1:])

    barrier = pltpu.get_barrier_semaphore()
    for dx, dy in SIDES:

        @pl.when(exists(dx, dy))
        def _(dx=dx, dy=dy):
            pl.semaphore_signal(
                barrier,
                inc=1,
                device_id=(me_wide + dx, me_narrow + dy),
                device_id_type=pl.DeviceIdType.MESH,
            )

    put(e_vol, [vol[x] for x in range(xs)], c1)
    put(e_cot, [cot[x] for x in range(xs)], c1)
    across = 1 + (me_wide > 0).astype(jnp.int32) + (me_wide < wide_count - 1).astype(jnp.int32)
    along = 1 + (me_narrow > 0).astype(jnp.int32) + (me_narrow < narrow_count - 1).astype(jnp.int32)
    pl.semaphore_wait(barrier, across * along - 1)

    send(*spec_vol)
    send(*spec_cot)

    receive(*spec_vol)
    hidden = []
    for x, pre in enumerate(conv(w_first, e_vol, xs, 1)):
        pre_first[x] = pre
        hidden.append(silu(pre).astype(BF))
        hidden_first[x] = hidden[-1]
    pooled = block_sum([h.astype(F32) for h in hidden], c1, 1)
    put(e_p1, [p * 0.125 for p in pooled], c1)
    send(*spec_p1)

    receive(*spec_cot)
    joined = [g.astype(BF) for g in conv(b_final, e_cot, xs, 1)]
    for x in range(xs):
        grad_joined[x] = joined[x]
    joined_sum = block_sum([g.astype(F32) for g in joined], c1, 1)

    receive(*spec_p1)
    hidden = []
    for x, pre in enumerate(conv(w_second, e_p1, x2, 2)):
        pre_second[x] = pre
        hidden.append(silu(pre).astype(BF))
        hidden_second[x] = hidden[-1]
    pooled = block_sum([h.astype(F32) for h in hidden], c2, 2)
    put(e_p2, [p * 0.125 for p in pooled], c2)
    send(*spec_p2)

    receive(*spec_p2)
    pre_bottom = conv(w_bottom, e_p2, x3, 4)
    lifted = []
    for pre in pre_bottom:
        hid = silu(pre).astype(BF)
        lifted.append(
            jnp.concatenate(
                [
                    jnp.dot(lift[...], hid[y * c3 : (y + 1) * c3], preferred_element_type=F32)
                    for y in range(y3)
                ],
                axis=0,
            )
        )
    lifted = spread(lifted, c2)
    put(e_j2, [lifted[x] + hidden_second[x].astype(F32) for x in range(x2)], c2)
    send(*spec_j2)

    receive(*spec_j2)
    pre_decode = conv(w_decode, e_j2, x2, 2)
    put(e_gd, [joined_sum[x] * slope(pre_decode[x]) for x in range(x2)], c1)
    send(*spec_gd)
    decoded = spread([silu(pre).astype(BF).astype(F32) for pre in pre_decode], c1)
    put(e_j1, [decoded[x] + hidden_first[x].astype(F32) for x in range(xs)], c1)
    send(*spec_j1)

    receive(*spec_gd)
    second_up = [g.astype(BF).astype(F32) for g in conv(b_decode, e_gd, x2, 2)]
    grad_lift = [g.astype(BF) for g in block_sum(second_up, c2, 2)]
    grad_bottom = []
    for x in range(x3):
        back = jnp.concatenate(
            [
                jnp.dot(
                    lift_t[...],
                    grad_lift[x][y * c2 : (y + 1) * c2],
                    preferred_element_type=F32,
                )
                for y in range(y3)
            ],
            axis=0,
        )
        grad_bottom.append(back * slope(pre_bottom[x]))
    put(e_gb, grad_bottom, c3)
    send(*spec_gb)

    receive(*spec_j1)
    for x, out in enumerate(conv(w_final, e_j1, xs, 1)):
        features_ref[x] = out.astype(BF)

    receive(*spec_gb)
    pool_second = spread(conv(b_bottom, e_gb, x3, 4), c2)
    put(
        e_gs,
        [(second_up[x] + pool_second[x] * 0.125) * slope(pre_second[x]) for x in range(x2)],
        c2,
    )
    send(*spec_gs)

    receive(*spec_gs)
    pool_first = spread(conv(b_second, e_gs, x2, 2), c1)
    put(
        e_gf,
        [
            (grad_joined[x].astype(F32) + pool_first[x] * 0.125) * slope(pre_first[x])
            for x in range(xs)
        ],
        c1,
    )
    send(*spec_gf)

    receive(*spec_gf)
    for x, out in enumerate(conv(b_first, e_gf, xs, 1)):
        grad_ref[x] = out.astype(BF)

    for index, edged, nx, ny, width in started:
        for side, (dx, dy) in enumerate(SIDES):
            copy = copy_of(index, edged, side, nx, ny, width)
            pl.when(exists(dx, dy))(copy.wait_send)


def flipped(kernel):
    return jnp.flip(kernel, (0, 1, 2)).transpose(0, 1, 2, 4, 3)


def banded(kernel, ys):
    outs, ins = kernel.shape[4], kernel.shape[3]
    turned = kernel.transpose(2, 4, 0, 1, 3)
    stacked = jnp.stack(
        [
            jnp.pad(turned, ((0, 0), (0, 0), (0, 0), (y, ys - 1 - y), (0, 0)))
            for y in range(ys)
        ],
        axis=1,
    )
    return stacked.reshape(3 * ys * outs, 3 * (ys + 2) * ins)


def shards(
    wide_count, narrow_count,
    volume, cotangent, conv_first, conv_second, conv_bottom, lift_weight, conv_decode, conv_final
):
    c1, xs, ys, lanes = volume.shape
    c2, c3 = lift_weight.shape
    x2, y2, x3, y3 = xs // 2, ys // 2, xs // 4, ys // 4

    def columns(field):
        return field.transpose(1, 2, 0, 3).reshape(xs, ys * c1, lanes)

    def back(field):
        return field.reshape(xs, ys, c1, lanes).transpose(2, 0, 1, 3)

    def edged(nx, ny, width):
        return pltpu.VMEM((nx + 2, (ny + 2) * width, lanes), BF)

    shape = jax.ShapeDtypeStruct((xs, ys * c1, lanes), BF)
    vmem = pl.BlockSpec(memory_space=pltpu.VMEM)
    call = pl.pallas_call(
        functools.partial(body, wide_count, narrow_count, xs, ys, (c1, c2, c3)),
        out_shape=(shape, shape),
        in_specs=[vmem] * 14,
        out_specs=(vmem, vmem),
        scratch_shapes=[
            edged(xs, ys, c1),
            edged(xs, ys, c1),
            edged(x2, y2, c1),
            edged(x3, y3, c2),
            edged(x2, y2, c2),
            edged(xs, ys, c1),
            edged(x2, y2, c1),
            edged(x3, y3, c3),
            edged(x2, y2, c2),
            edged(xs, ys, c1),
            pltpu.VMEM((xs, ys * c1, lanes), F32),
            pltpu.VMEM((xs, ys * c1, lanes), BF),
            pltpu.VMEM((xs, ys * c1, lanes), BF),
            pltpu.VMEM((x2, y2 * c2, lanes), F32),
            pltpu.VMEM((x2, y2 * c2, lanes), BF),
            pltpu.SemaphoreType.DMA((10, 8)),
            pltpu.SemaphoreType.DMA((10, 8)),
        ],
        compiler_params=pltpu.CompilerParams(
            collective_id=0, has_side_effects=True, vmem_limit_bytes=40 * 1024 * 1024
        ),
    )
    features, grad = call(
        columns(volume),
        columns(cotangent),
        banded(conv_first, ys),
        banded(conv_second, y2),
        banded(conv_bottom, y3),
        lift_weight,
        lift_weight.T,
        banded(conv_decode, y2),
        banded(conv_final, ys),
        banded(flipped(conv_first), ys),
        banded(flipped(conv_second), y2),
        banded(flipped(conv_bottom), y3),
        banded(flipped(conv_decode), y2),
        banded(flipped(conv_final), ys),
    )
    return back(features), back(grad)


def solution(mesh):
    cells = P(None, "wide", "narrow", None)
    return jax.shard_map(
        functools.partial(shards, mesh.shape["wide"], mesh.shape["narrow"]),
        mesh=mesh,
        in_specs=(cells, cells, P(), P(), P(), P(), P(), P()),
        out_specs=(cells, cells),
        check_vma=False,
    )
```

time: 219 us -> 88.5 us (0.40)
  starting transfers between devices: 111 us -> 0 us
  Pallas kernels: 0 us -> 38.7 us
  waiting for transfers between devices: 37.2 us -> 0 us
  matrix products: 16.4 us -> 0 us
  other arithmetic: 7.22 us -> 2.38 us
    ppermute x40 -> x0, starting transfers between devices: 111 us -> none  [the longest x20 56.8 us: extended(): lax.ppermute(tail, axis, [(i, (i + 1) % count) for i in range(ends)])]
    pallas_call x0 -> x1, Pallas kernels: none -> 38.7 us  [shards(): call(columns(volume), columns(cotangent), banded(conv_first, ys), banded(...]
    ppermute x40 -> x0, waiting for transfers between devices: 37.2 us -> none  [the longest x20 30 us: extended(): lax.ppermute(head, axis, [((i + 1) % count, i) for i in range(ends)])]
    conv_general_dilated x33 -> x0, local copies, waits for them, and re-layouts: 29 us -> none  [conv_valid(): lax.conv_general_dilated(padded[None], kernel, (1, 1, 1), 'VALID', dimens...]
    reshape x0 -> x14, local copies, waits for them, and re-layouts: none -> 21.6 us  [banded(): return stacked.reshape(3 * ys * outs, 3 * (ys + 2) * ins)]
    conv_general_dilated x10 -> x0, matrix products: 16.1 us -> none  [conv_valid(): lax.conv_general_dilated(padded[None], kernel, (1, 1, 1), 'VALID', dimens...]
    another operation x0 -> x21, local copies, waits for them, and re-layouts: none -> 16.1 us  [the longest x3 7.28 us: banded(): return stacked.reshape(3 * ys * outs, 3 * (ys + 2) * ins)]
    broadcast_in_dim x10 -> x0, other arithmetic: 5.02 us -> none  [conv_valid(): padded[None]]
  transfers between devices with their start and end apart: 40 -> 0, of which waited for: 15 -> 0; matrix products, arithmetic and copies ran while one was open for 14% -> 0% of each run, Pallas kernels for 0% -> 0%
where the time goes in v1:
time: 88.5 us; the launch traced here: 87.6 us
  local copies, waits for them, and re-layouts  45.6 us (52%)
  Pallas kernels  38.7 us (44%)
  other arithmetic  2.38 us (3%)
  between operations  1 us (1%)
    pallas_call x1, Pallas kernels, shards(): call(columns(volume), columns(cotangent), banded(conv_first, ys), banded(...  38.7 us
    reshape x14, local copies, waits for them, and re-layouts, banded(): return stacked.reshape(3 * ys * outs, 3 * (ys + 2) * ins)  21.6 us
    another operation x3, local copies, waits for them, and re-layouts, banded(): return stacked.reshape(3 * ys * outs, 3 * (ys + 2) * ins)  7.28 us
    another operation x12, local copies, waits for them, and re-layouts, banded(): jnp.stack([jnp.pad(turned, ((0, 0), (0, 0), (0, 0), (y, ys - 1 - y), (0,...  6.56 us
    unnamed x23, local copies, waits for them, and re-layouts  3.88 us
    transpose x2, local copies, waits for them, and re-layouts, columns(): return field.transpose(1, 2, 0, 3).reshape(xs, ys * c1, lanes)  3.19 us
    another operation x8, other arithmetic, banded(): jnp.stack([jnp.pad(turned, ((0, 0), (0, 0), (0, 0), (y, ys - 1 - y), (0,...  2.38 us
    another operation x6, local copies, waits for them, and re-layouts, banded(): turned = kernel.transpose(2, 4, 0, 1, 3)  2.24 us

profile of v1, /device:TPU:4, one launch (start us, length us, event | category | flops | bytes accessed | tf_op | source)
XLA Modules:
  0.0 87.6 jit_solution(16345405652093797482)
XLA Ops:
  0.6 1.0 %reverse_bitcast_fusion.4 = bf16[3,32,3,3,32]{4,1,0,3,2:T(8,128)(2,1)S(1)} fusion(bf16[3,3,3,32,32]{4,3,2,1,0:T(8,128)(2,1)} %param.10), kind=kLoop, calls=%fused_computation.36 | loop fusion | bytes 110592 | tf_op jit(solution)/shard_map/transpose;transpose | solution.py:304
  1.6 0.3 pad_bitcast_fusion.7
  1.9 0.5 pad_maximum_fusion.2
  2.4 0.8 copy.50
  3.1 0.0 copy-start.9
  3.1 1.4 %reshape.55.b_first = bf16[384,576]{1,0:T(8,128)(2,1)S(1)} reshape(bf16[3,4,32,3,6,32]{5,4,3,2,1,0:T(8,128)(2,1)S(1)} %copy.50) | data formatting | bytes 884736 | tf_op jit(solution)/shard_map/reshape | solution.py:312
  4.5 0.0 copy-done.9
  4.6 0.3 pad_bitcast_fusion.3
  4.9 0.5 pad_maximum_fusion.3
  5.4 0.8 copy.51
  6.1 1.4 %reshape.56.b_final = bf16[384,576]{1,0:T(8,128)(2,1)S(1)} reshape(bf16[3,4,32,3,6,32]{5,4,3,2,1,0:T(8,128)(2,1)S(1)} %copy.51) | data formatting | bytes 884736 | tf_op jit(solution)/shard_map/reshape | solution.py:312
  7.5 1.9 %pad_bitcast_fusion.11 = (bf16[3,1,32,3,6,32]{2,5,0,4,3,1:T(8,128)(2,1)S(1)}, bf16[3,1,32,3,6,32]{2,5,0,4,3,1:T(8,128)(2,1)S(1)}, bf16[3,1,32,3,6,32]{2,5,0,4,3,...) fusion(bf16[3,32,3,3,32]{1,4,0,3,2:T(8,128)(2,1)} %bitcast.86), kind=kLoop, calls=%fused_computation.20 | loop fusion | bytes 497664 | tf_op jit(solution)/shard_map/stack | solution.py:305
  9.4 0.5 pad_maximum_fusion.1
  9.9 2.6 %copy.49 = bf16[3,4,32,3,6,32]{5,4,3,2,1,0:T(8,128)(2,1)} copy(bf16[3,4,32,3,6,32]{2,5,0,4,3,1:T(8,128)(2,1)S(1)} %pad_maximum_fusion.1) | data formatting | bytes 884736 | tf_op jit(solution)/shard_map/reshape | solution.py:312
  12.5 0.0 copy-start.10
  12.5 3.3 %reshape.54.w_final = bf16[384,576]{1,0:T(8,128)(2,1)S(1)} reshape(bf16[3,4,32,3,6,32]{5,4,3,2,1,0:T(8,128)(2,1)} %copy.49) | data formatting | bytes 884736 | tf_op jit(solution)/shard_map/reshape | solution.py:312
  15.7 0.0 copy-done.10
  15.7 0.3 pad_bitcast_fusion.15
  16.0 0.5 pad_maximum_fusion
  16.5 2.6 %copy.47 = bf16[3,4,32,3,6,32]{5,4,3,2,1,0:T(8,128)(2,1)} copy(bf16[3,4,32,3,6,32]{2,5,0,4,3,1:T(8,128)(2,1)S(1)} %pad_maximum_fusion) | data formatting | bytes 884736 | tf_op jit(solution)/shard_map/reshape | solution.py:312
  19.1 0.0 copy-start.7
  19.1 3.3 %reshape.52.w_first = bf16[384,576]{1,0:T(8,128)(2,1)S(1)} reshape(bf16[3,4,32,3,6,32]{5,4,3,2,1,0:T(8,128)(2,1)} %copy.47) | data formatting | bytes 884736 | tf_op jit(solution)/shard_map/reshape | solution.py:312
  22.4 0.0 copy-done.7
  22.4 0.1 pad_bitcast_fusion.17
  22.5 0.0 copy-start.6
  22.5 0.1 pad_maximum_fusion.7
  22.7 0.6 copy.36
  23.3 0.4 reshape.48
  23.7 0.9 %copy.43.b_decode = bf16[384,384]{1,0:T(8,128)(2,1)} copy(bf16[384,384]{0,1:T(8,128)(2,1)S(1)} %reshape.48) | data formatting | bytes 589824 | tf_op jit(solution)/shard_map/reshape | solution.py:312
  24.6 0.0 copy-done.6
  24.6 0.1 pad_bitcast_fusion.19
  24.7 0.1 pad_maximum_fusion.6
  24.8 0.3 copy.34
  25.1 0.4 reshape.47.b_second
  25.5 0.1 pad_bitcast_fusion.23
  25.6 0.0 copy-start.8
  25.6 0.1 pad_maximum_fusion.4
  25.7 1.4 %copy.28 = bf16[3,2,64,3,4,32]{2,1,0,5,4,3:T(2,128)(2,1)} copy(bf16[3,2,64,3,4,32]{2,5,0,4,3,1:T(8,128)(2,1)S(1)} %pad_maximum_fusion.4) | data formatting | bytes 589824 | tf_op jit(solution)/shard_map/stack | solution.py:305
  27.2 1.5 %reshape.43 = bf16[384,384]{0,1:T(8,128)(2,1)S(1)} reshape(bf16[3,2,64,3,4,32]{2,1,0,5,4,3:T(2,128)(2,1)} %copy.28) | data formatting | bytes 589824 | tf_op jit(solution)/shard_map/reshape | solution.py:312
  28.7 0.9 %copy.39.w_second = bf16[384,384]{1,0:T(8,128)(2,1)} copy(bf16[384,384]{0,1:T(8,128)(2,1)S(1)} %reshape.43) | data formatting | bytes 589824 | tf_op jit(solution)/shard_map/reshape | solution.py:312
  29.6 0.0 copy-done.8
  29.6 0.1 pad_bitcast_fusion.21
  29.7 0.1 pad_maximum_fusion.5
  29.8 1.1 %copy.31 = bf16[3,2,32,3,4,64]{5,4,3,2,1,0:T(4,128)(2,1)} copy(bf16[3,2,32,3,4,64]{5,2,0,4,3,1:T(8,128)(2,1)S(1)} %pad_maximum_fusion.5) | data formatting | bytes 589824 | tf_op jit(solution)/shard_map/stack | solution.py:305
  31.0 1.5 %reshape.44.w_decode = bf16[192,768]{1,0:T(8,128)(2,1)S(1)} reshape(bf16[3,2,32,3,4,64]{5,4,3,2,1,0:T(4,128)(2,1)} %copy.31) | data formatting | bytes 589824 | tf_op jit(solution)/shard_map/reshape | solution.py:312
  32.5 0.0 copy-start.5
  32.5 3.3 %copy.48 = bf16[3,128,3,3,64]{4,3,2,1,0:T(4,128)(2,1)} copy(bf16[3,128,3,3,64]{1,4,0,3,2:T(8,128)(2,1)} %bitcast.83) | data formatting | bytes 884736 | tf_op jit(solution)/shard_map/reshape;stack | solution.py:312
  35.8 2.5 %reshape.53.w_bottom = bf16[384,576]{1,0:T(8,128)(2,1)S(1)} reshape(bf16[3,128,3,3,64]{4,3,2,1,0:T(4,128)(2,1)} %copy.48) | data formatting | bytes 884736 | tf_op jit(solution)/shard_map/reshape;stack | solution.py:312
  38.3 0.0 copy-done.5
  38.3 0.0 copy-start.4
  38.4 1.2 %copy.35 = bf16[3,64,3,3,128]{4,3,2,1,0:T(4,128)(2,1)} copy(bf16[3,64,3,3,128]{4,1,0,3,2:T(8,128)(2,1)S(1)} %reverse_bitcast_fusion) | data formatting | bytes 884736 | tf_op jit(solution)/shard_map/transpose;transpose | solution.py:304
  39.6 1.5 %reshape_stack.7.b_bottom = bf16[192,1152]{1,0:T(8,128)(2,1)S(1)} reshape(bf16[3,64,3,3,128]{4,3,2,1,0:T(4,128)(2,1)} %copy.35) | data formatting | bytes 884736 | tf_op jit(solution)/shard_map/reshape;stack | solution.py:312
  41.0 1.6 %copy.25 = bf16[4,4,32,128]{3,2,1,0:T(8,128)(2,1)} copy(bf16[4,4,32,128]{3,1,0,2:T(4,128)(2,1)} %bitcast.88) | data formatting | bytes 262144 | tf_op jit(solution)/shard_map/transpose | solution.py:324
  42.6 1.6 %copy.26 = bf16[4,4,32,128]{3,2,1,0:T(8,128)(2,1)} copy(bf16[4,4,32,128]{3,1,0,2:T(4,128)(2,1)} %bitcast.89) | data formatting | bytes 262144 | tf_op jit(solution)/shard_map/transpose | solution.py:324
  44.2 0.0 copy-done.4
  44.2 0.1 copy.30
  44.4 0.0 copy-start
  44.4 1.0 %copy-done = bf16[384,384]{1,0:T(8,128)(2,1)S(1)} copy-done((bf16[384,384]{1,0:T(8,128)(2,1)S(1)}, bf16[384,384]{1,0:T(8,128)(2,1)}, u32[]{:S(2)}) %copy-start) | copy-done | bytes 294936
  45.3 0.0 copy-start.1
  45.3 1.0 %copy-done.1 = bf16[384,384]{1,0:T(8,128)(2,1)S(1)} copy-done((bf16[384,384]{1,0:T(8,128)(2,1)S(1)}, bf16[384,384]{1,0:T(8,128)(2,1)}, u32[]{:S(2)}) %copy-start.1) | copy-done | bytes 294936
  46.3 0.9 %copy-done.2 = bf16[4,4,32,128]{3,2,1,0:T(8,128)(2,1)S(1)} copy-done((bf16[4,4,32,128]{3,2,1,0:T(8,128)(2,1)S(1)}, bf16[4,4,32,128]{3,2,1,0:T(8,128)(2,1)}, u32[]{:S(2)}) %copy-start.2) | copy-done | bytes 131096
  47.2 0.9 %copy-done.3 = bf16[4,4,32,128]{3,2,1,0:T(8,128)(2,1)S(1)} copy-done((bf16[4,4,32,128]{3,2,1,0:T(8,128)(2,1)S(1)}, bf16[4,4,32,128]{3,2,1,0:T(8,128)(2,1)}, u32[]{:S(2)}) %copy-start.3) | copy-done | bytes 131096
  48.1 38.7 %shard_map.95 = (bf16[4,128,128]{2,1,0:T(8,128)(2,1)S(1)}, bf16[4,128,128]{2,1,0:T(8,128)(2,1)S(1)}) custom-call(bf16[4,128,128]{2,1,0:T(8,128)(2,1)S(1)} %bitcast.78, bf16[4,128,128]{2,1,0:T(8,128)(2,1)S(1)} %bitcast.79, bf16[384,576]{1,0:T(8,128)(2,1)S(1)} %reshape.52.w_first, bf16[384,384]{1,0:T(8,128)(2,1)S(1)} %copy-done.1, ...), custom_call_target="tpu_custom_call" | custom-call | tf_op jit(solution)/shard_map/pallas_call | solution.py:362
  86.8 0.8 copy_bitcast_fusion
  (6 shorter events, 0.1 us)
Async XLA Ops:
  3.1 1.4 %copy-start.9 = (bf16[3,3,3,32,32]{4,3,2,1,0:T(8,128)(2,1)S(1)}, bf16[3,3,3,32,32]{4,3,2,1,0:T(8,128)(2,1)}, u32[]{:S(2)}) copy-start(bf16[3,3,3,32,32]{4,3,2,1,0:T(8,128)(2,1)} %param.15) | copy-start | bytes 165892
  12.5 3.3 %copy-start.10 = (bf16[3,3,3,32,32]{4,3,2,1,0:T(8,128)(2,1)S(1)}, bf16[3,3,3,32,32]{4,3,2,1,0:T(8,128)(2,1)}, u32[]{:S(2)}) copy-start(bf16[3,3,3,32,32]{4,3,2,1,0:T(8,128)(2,1)} %param.10) | copy-start | bytes 165892
  19.1 3.3 %copy-start.7 = (bf16[3,3,3,64,32]{3,4,2,1,0:T(8,128)(2,1)S(1)}, bf16[3,3,3,64,32]{3,4,2,1,0:T(8,128)(2,1)}, u32[]{:S(2)}) copy-start(bf16[3,3,3,64,32]{3,4,2,1,0:T(8,128)(2,1)} %param.14) | copy-start | bytes 331780
  22.5 2.1 %copy-start.6 = (bf16[3,3,3,32,64]{4,3,2,1,0:T(8,128)(2,1)S(1)}, bf16[3,3,3,32,64]{4,3,2,1,0:T(8,128)(2,1)}, u32[]{:S(2)}) copy-start(bf16[3,3,3,32,64]{4,3,2,1,0:T(8,128)(2,1)} %param.11) | copy-start | bytes 331780
  25.6 4.0 %copy-start.8 = (bf16[3,3,3,64,32]{3,4,2,1,0:T(8,128)(2,1)S(1)}, bf16[3,3,3,64,32]{3,4,2,1,0:T(8,128)(2,1)}, u32[]{:S(2)}) copy-start(bf16[3,3,3,64,32]{3,4,2,1,0:T(8,128)(2,1)} %param.14) | copy-start | bytes 331780
  32.5 5.9 %copy-start.5 = (bf16[3,3,3,64,128]{4,3,2,1,0:T(8,128)(2,1)S(1)}, bf16[3,3,3,64,128]{4,3,2,1,0:T(8,128)(2,1)}, u32[]{:S(2)}) copy-start(bf16[3,3,3,64,128]{4,3,2,1,0:T(8,128)(2,1)} %param.12) | copy-start | bytes 1327108
  38.3 5.9 %copy-start.4 = (bf16[64,128]{1,0:T(8,128)(2,1)S(1)}, bf16[64,128]{1,0:T(8,128)(2,1)}, u32[]{:S(2)}) copy-start(bf16[64,128]{1,0:T(8,128)(2,1)} %lift.1) | copy-start | bytes 49156
  44.4 1.0 %copy-start = (bf16[384,384]{1,0:T(8,128)(2,1)S(1)}, bf16[384,384]{1,0:T(8,128)(2,1)}, u32[]{:S(2)}) copy-start(bf16[384,384]{1,0:T(8,128)(2,1)} %copy.43.b_decode) | copy-start | bytes 884740
  45.3 1.0 %copy-start.1 = (bf16[384,384]{1,0:T(8,128)(2,1)S(1)}, bf16[384,384]{1,0:T(8,128)(2,1)}, u32[]{:S(2)}) copy-start(bf16[384,384]{1,0:T(8,128)(2,1)} %copy.39.w_second) | copy-start | bytes 884740
  46.3 0.9 %copy-start.2 = (bf16[4,4,32,128]{3,2,1,0:T(8,128)(2,1)S(1)}, bf16[4,4,32,128]{3,2,1,0:T(8,128)(2,1)}, u32[]{:S(2)}) copy-start(bf16[4,4,32,128]{3,2,1,0:T(8,128)(2,1)} %copy.25) | copy-start | bytes 393220
  47.2 0.9 %copy-start.3 = (bf16[4,4,32,128]{3,2,1,0:T(8,128)(2,1)S(1)}, bf16[4,4,32,128]{3,2,1,0:T(8,128)(2,1)}, u32[]{:S(2)}) copy-start(bf16[4,4,32,128]{3,2,1,0:T(8,128)(2,1)} %copy.26) | copy-start | bytes 393220

commit v2 on v1

--- a/solution.py
+++ b/solution.py
@@ -83,7 +83,7 @@
 
 def body(
     wide_count, narrow_count, xs, ys, chans,
-    vol, cot, w_first, w_second, w_bottom, lift, lift_t, w_decode, w_final,
+    vol, cot, w_first, w_second, w_bottom, lift, w_decode, w_final,
     b_first, b_second, b_bottom, b_decode, b_final,
     features_ref, grad_ref,
     e_vol, e_cot, e_p1, e_p2, e_j2, e_j1, e_gd, e_gb, e_gs, e_gf,
@@ -247,9 +247,10 @@
     for x in range(x3):
         back = jnp.concatenate(
             [
-                jnp.dot(
-                    lift_t[...],
+                lax.dot_general(
+                    lift[...],
                     grad_lift[x][y * c2 : (y + 1) * c2],
+                    (((0,), (0,)), ((), ())),
                     preferred_element_type=F32,
                 )
                 for y in range(y3)
@@ -295,21 +296,72 @@
             pl.when(exists(dx, dy))(copy.wait_send)
 
 
-def flipped(kernel):
-    return jnp.flip(kernel, (0, 1, 2)).transpose(0, 1, 2, 4, 3)
-
-
-def banded(kernel, ys):
-    outs, ins = kernel.shape[4], kernel.shape[3]
-    turned = kernel.transpose(2, 4, 0, 1, 3)
-    stacked = jnp.stack(
-        [
-            jnp.pad(turned, ((0, 0), (0, 0), (0, 0), (y, ys - 1 - y), (0, 0)))
-            for y in range(ys)
-        ],
-        axis=1,
-    )
-    return stacked.reshape(3 * ys * outs, 3 * (ys + 2) * ins)
+def forward_matrix(kernel, ys, ins, outs):
+    zero = jnp.zeros((ins, outs), BF)
+    strips = []
+    for ex in range(3):
+        for rim in range(ys + 2):
+            strips.append(
+                jnp.concatenate(
+                    [
+                        kernel[pl.ds(((ex * 3 + rim - y) * 3 + ez) * ins, ins), :]
+                        if 0 <= rim - y < 3
+                        else zero
+                        for ez in range(3)
+                        for y in range(ys)
+                    ],
+                    axis=1,
+                )
+            )
+    turned = jnp.concatenate(strips, axis=0)
+    size = 3 * ys * outs
+    row = lax.broadcasted_iota(jnp.int32, (size, size), 0)
+    column = lax.broadcasted_iota(jnp.int32, (size, size), 1)
+    eye = jnp.where(row == column, 1.0, 0.0).astype(BF)
+    return lax.dot_general(
+        eye, turned, (((1,), (1,)), ((), ())), preferred_element_type=F32
+    ).astype(BF)
+
+
+def backward_strips(kernel, ys, outs, ins):
+    zero = jnp.zeros((outs, ins), BF)
+    return [
+        jnp.concatenate(
+            [
+                kernel[pl.ds((((2 - ex) * 3 + 2 - rim + y) * 3 + 2 - ez) * outs, outs), :]
+                if 0 <= rim - y < 3
+                else zero
+                for ex in range(3)
+                for rim in range(ys + 2)
+            ],
+            axis=1,
+        )
+        for ez in range(3)
+        for y in range(ys)
+    ]
+
+
+def prepare(
+    xs, ys, chans, vol, cot, first, second, bottom, decode, final,
+    vol_out, cot_out, w_first, w_second, w_bottom, w_decode, w_final,
+    b_first, b_second, b_bottom, b_decode, b_final,
+):
+    c1, c2, c3 = chans
+    y2, y3 = ys // 2, ys // 4
+    for field, out in ((vol, vol_out), (cot, cot_out)):
+        for x in range(xs):
+            for y in range(ys):
+                out[x, y * c1 : (y + 1) * c1, :] = field[:, x, y, :]
+    for kernel, ahead, behind, count, ins, outs in (
+        (first, w_first, b_first, ys, c1, c1),
+        (second, w_second, b_second, y2, c1, c2),
+        (bottom, w_bottom, b_bottom, y3, c2, c3),
+        (decode, w_decode, b_decode, y2, c2, c1),
+        (final, w_final, b_final, ys, c1, c1),
+    ):
+        ahead[...] = forward_matrix(kernel, count, ins, outs)
+        for place, strip in enumerate(backward_strips(kernel, count, ins, outs)):
+            behind[place * ins : (place + 1) * ins, :] = strip
 
 
 def shards(
@@ -320,9 +372,6 @@
     c2, c3 = lift_weight.shape
     x2, y2, x3, y3 = xs // 2, ys // 2, xs // 4, ys // 4
 
-    def columns(field):
-        return field.transpose(1, 2, 0, 3).reshape(xs, ys * c1, lanes)
-
     def back(field):
         return field.reshape(xs, ys, c1, lanes).transpose(2, 0, 1, 3)
 
@@ -334,7 +383,7 @@
     call = pl.pallas_call(
         functools.partial(body, wide_count, narrow_count, xs, ys, (c1, c2, c3)),
         out_shape=(shape, shape),
-        in_specs=[vmem] * 14,
+        in_specs=[vmem] * 13,
         out_specs=(vmem, vmem),
         scratch_shapes=[
             edged(xs, ys, c1),
@@ -359,21 +408,25 @@
             collective_id=0, has_side_effects=True, vmem_limit_bytes=40 * 1024 * 1024
         ),
     )
+    kernels = (conv_first, conv_second, conv_bottom, conv_decode, conv_final)
+    counts = (ys, y2, y3, y2, ys)
+
+    def matrix(count, ins, outs):
+        return jax.ShapeDtypeStruct((3 * count * outs, 3 * (count + 2) * ins), BF)
+
+    prepared = pl.pallas_call(
+        functools.partial(prepare, xs, ys, (c1, c2, c3)),
+        out_shape=(shape, shape)
+        + tuple(matrix(n, k.shape[3], k.shape[4]) for n, k in zip(counts, kernels))
+        + tuple(matrix(n, k.shape[4], k.shape[3]) for n, k in zip(counts, kernels)),
+        in_specs=[vmem] * 7,
+        out_specs=(vmem,) * 12,
+        compiler_params=pltpu.CompilerParams(vmem_limit_bytes=40 * 1024 * 1024),
+    )(volume, cotangent, *(k.reshape(27 * k.shape[3], k.shape[4]) for k in kernels))
+    (vol, cot, w_first, w_second, w_bottom, w_decode, w_final) = prepared[:7]
     features, grad = call(
-        columns(volume),
-        columns(cotangent),
-        banded(conv_first, ys),
-        banded(conv_second, y2),
-        banded(conv_bottom, y3),
-        lift_weight,
-        lift_weight.T,
-        banded(conv_decode, y2),
-        banded(conv_final, ys),
-        banded(flipped(conv_first), ys),
-        banded(flipped(conv_second), y2),
-        banded(flipped(conv_bottom), y3),
-        banded(flipped(conv_decode), y2),
-        banded(flipped(conv_final), ys),
+        vol, cot, w_first, w_second, w_bottom, lift_weight, w_decode, w_final,
+        *prepared[7:],
     )
     return back(features), back(grad)
 

time: 88.5 us -> 48.2 us (0.54)
  local copies, waits for them, and re-layouts: 45.6 us -> 6.47 us
  other arithmetic: 2.38 us -> 0 us
  Pallas kernels: 38.7 us -> 40.5 us
    reshape x14 -> x0, local copies, waits for them, and re-layouts: 21.6 us -> none  [banded(): return stacked.reshape(3 * ys * outs, 3 * (ys + 2) * ins)]
    another operation x21 -> x0, local copies, waits for them, and re-layouts: 16.1 us -> none  [the longest x3 7.28 us: banded(): return stacked.reshape(3 * ys * outs, 3 * (ys + 2) * ins)]
    transpose x2 -> x0, local copies, waits for them, and re-layouts: 3.19 us -> none  [columns(): return field.transpose(1, 2, 0, 3).reshape(xs, ys * c1, lanes)]
    another operation x8 -> x0, other arithmetic: 2.38 us -> none  [banded(): jnp.stack([jnp.pad(turned, ((0, 0), (0, 0), (0, 0), (y, ys - 1 - y), (0,...]
    pallas_call x1 -> x2, Pallas kernels: 38.7 us -> 40.5 us  [the longest x1 38.7 us: shards(): call(vol, cot, w_first, w_second, w_bottom, lift_weight, w_decode, w_fina...]
    unnamed x23 -> x15, local copies, waits for them, and re-layouts: 3.88 us -> 5.63 us
where the time goes in v2:
time: 48.2 us; the launch traced here: 47.7 us
  Pallas kernels  40.5 us (84%)
  local copies, waits for them, and re-layouts  6.47 us (13%)
  between operations  0.7 us (1%)
    pallas_call x1, Pallas kernels, shards(): call(vol, cot, w_first, w_second, w_bottom, lift_weight, w_decode, w_fina...  38.7 us
    unnamed x15, local copies, waits for them, and re-layouts  5.63 us
    pallas_call x1, Pallas kernels, shards(): pl.pallas_call(functools.partial(prepare, xs, ys, (c1, c2, c3)), out_shap...  1.83 us

profile of v2, /device:TPU:4, one launch (start us, length us, event | category | flops | bytes accessed | tf_op | source)
XLA Modules:
  0.0 47.7 jit_solution(123330167159378237)
XLA Ops:
  0.6 0.0 copy-start
  0.6 0.0 copy-start.1
  0.7 1.2 %copy.10 = bf16[3,3,3,64,32]{4,3,2,1,0:T(8,128)(2,1)S(1)} copy(bf16[3,3,3,64,32]{3,4,2,1,0:T(8,128)(2,1)} %param.14) | data formatting | bytes 221184 | tf_op args[6]
  1.9 0.0 copy-done
  1.9 0.0 copy-done.1
  1.9 0.0 copy-start.2
  1.9 0.9 %copy-done.2 = bf16[3,3,3,32,64]{4,3,2,1,0:T(8,128)(2,1)S(1)} copy-done((bf16[3,3,3,32,64]{4,3,2,1,0:T(8,128)(2,1)S(1)}, bf16[3,3,3,32,64]{4,3,2,1,0:T(8,128)(2,1)}, u32[]{:S(2)}) %copy-start.2) | copy-done | bytes 110616
  2.9 0.0 copy-start.3
  2.9 0.9 %copy-done.3 = bf16[3,3,3,32,32]{4,3,2,1,0:T(8,128)(2,1)S(1)} copy-done((bf16[3,3,3,32,32]{4,3,2,1,0:T(8,128)(2,1)S(1)}, bf16[3,3,3,32,32]{4,3,2,1,0:T(8,128)(2,1)}, u32[]{:S(2)}) %copy-start.3) | copy-done | bytes 55320
  3.8 0.0 copy-start.4
  3.8 0.9 %copy-done.4 = bf16[32,4,4,128]{3,2,1,0:T(4,128)(2,1)S(1)} copy-done((bf16[32,4,4,128]{3,2,1,0:T(4,128)(2,1)S(1)}, bf16[32,4,4,128]{3,2,1,0:T(4,128)(2,1)}, u32[]{:S(2)}) %copy-start.4) | copy-done | bytes 131096
  4.7 0.0 copy-start.5
  4.7 0.9 %copy-done.5 = bf16[32,4,4,128]{3,2,1,0:T(4,128)(2,1)S(1)} copy-done((bf16[32,4,4,128]{3,2,1,0:T(4,128)(2,1)S(1)}, bf16[32,4,4,128]{3,2,1,0:T(4,128)(2,1)}, u32[]{:S(2)}) %copy-start.5) | copy-done | bytes 131096
  5.6 1.8 %shard_map.95 = (bf16[4,128,128]{2,1,0:T(8,128)(2,1)S(1)}, bf16[4,128,128]{2,1,0:T(8,128)(2,1)S(1)}, bf16[384,576]{1,0:T(8,128)(2,1)S(1)}, bf16[384,384]{1,0:T(8...) custom-call(bf16[32,4,4,128]{3,2,1,0:T(4,128)(2,1)S(1)} %copy-done.4, ...), custom_call_target="tpu_custom_call" | custom-call | tf_op jit(solution)/shard_map/pallas_call | solution.py:417
  7.4 0.0 copy-start.6
  7.4 0.7 %copy-done.6 = bf16[64,128]{1,0:T(8,128)(2,1)S(1)} copy-done((bf16[64,128]{1,0:T(8,128)(2,1)S(1)}, bf16[64,128]{1,0:T(8,128)(2,1)}, u32[]{:S(2)}) %copy-start.6) | copy-done | bytes 16408
  8.2 38.7 %shard_map.96 = (bf16[4,128,128]{2,1,0:T(8,128)(2,1)S(1)}, bf16[4,128,128]{2,1,0:T(8,128)(2,1)S(1)}) custom-call(bf16[4,128,128]{2,1,0:T(8,128)(2,1)S(1)} %get-tuple-element.16.vol, bf16[4,128,128]{2,1,0:T(8,128)(2,1)S(1)} %get-tuple-element.17.cot, bf16[384,576]{1,0:T(8,128)(2,1)S(1)} %get-tuple-element.18.w_first, ...), custom_call_target="tpu_custom_call" | custom-call | tf_op jit(solution)/shard_map/pallas_call | solution.py:427
  46.9 0.8 %copy_bitcast_fusion = (bf16[32,4,4,128]{3,2,1,0:T(4,128)(2,1)}, bf16[32,4,4,128]{3,2,1,0:T(4,128)(2,1)}) fusion(bf16[4,4,32,128]{3,2,1,0:T(8,128)(2,1)S(1)} %bitcast.17, bf16[4,4,32,128]{3,2,1,0:T(8,128)(2,1)S(1)} %bitcast.16), kind=kLoop, calls=%fused_computation | loop fusion | bytes 524288 | tf_op jit(solution)/shard_map/transpose | solution.py:376
Async XLA Ops:
  0.6 1.3 %copy-start = (bf16[3,3,3,64,128]{4,3,2,1,0:T(8,128)(2,1)S(1)}, bf16[3,3,3,64,128]{4,3,2,1,0:T(8,128)(2,1)}, u32[]{:S(2)}) copy-start(bf16[3,3,3,64,128]{4,3,2,1,0:T(8,128)(2,1)} %param.12) | copy-start | bytes 1327108
  0.6 1.3 %copy-start.1 = (bf16[3,3,3,32,32]{4,3,2,1,0:T(8,128)(2,1)S(1)}, bf16[3,3,3,32,32]{4,3,2,1,0:T(8,128)(2,1)}, u32[]{:S(2)}) copy-start(bf16[3,3,3,32,32]{4,3,2,1,0:T(8,128)(2,1)} %param.10) | copy-start | bytes 165892
  1.9 0.9 %copy-start.2 = (bf16[3,3,3,32,64]{4,3,2,1,0:T(8,128)(2,1)S(1)}, bf16[3,3,3,32,64]{4,3,2,1,0:T(8,128)(2,1)}, u32[]{:S(2)}) copy-start(bf16[3,3,3,32,64]{4,3,2,1,0:T(8,128)(2,1)} %param.11) | copy-start | bytes 331780
  2.9 0.9 %copy-start.3 = (bf16[3,3,3,32,32]{4,3,2,1,0:T(8,128)(2,1)S(1)}, bf16[3,3,3,32,32]{4,3,2,1,0:T(8,128)(2,1)}, u32[]{:S(2)}) copy-start(bf16[3,3,3,32,32]{4,3,2,1,0:T(8,128)(2,1)} %param.15) | copy-start | bytes 165892
  3.8 0.9 %copy-start.4 = (bf16[32,4,4,128]{3,2,1,0:T(4,128)(2,1)S(1)}, bf16[32,4,4,128]{3,2,1,0:T(4,128)(2,1)}, u32[]{:S(2)}) copy-start(bf16[32,4,4,128]{3,2,1,0:T(4,128)(2,1)} %vol.1) | copy-start | bytes 393220
  4.7 0.9 %copy-start.5 = (bf16[32,4,4,128]{3,2,1,0:T(4,128)(2,1)S(1)}, bf16[32,4,4,128]{3,2,1,0:T(4,128)(2,1)}, u32[]{:S(2)}) copy-start(bf16[32,4,4,128]{3,2,1,0:T(4,128)(2,1)} %cot.1) | copy-start | bytes 393220
  7.4 0.7 %copy-start.6 = (bf16[64,128]{1,0:T(8,128)(2,1)S(1)}, bf16[64,128]{1,0:T(8,128)(2,1)}, u32[]{:S(2)}) copy-start(bf16[64,128]{1,0:T(8,128)(2,1)} %lift.1) | copy-start | bytes 49156

commit v3 on v1

--- a/solution.py
+++ b/solution.py
@@ -81,15 +81,75 @@
     return outs
 
 
+def tap(kernel, ex, ey, ez, rows, flip):
+    if flip:
+        ex, ey, ez = 2 - ex, 2 - ey, 2 - ez
+    return kernel[pl.ds(((ex * 3 + ey) * 3 + ez) * rows, rows), :]
+
+
+def turned(out, kernel, ys, rows, columns, flip):
+    zero = jnp.zeros((rows, columns), BF)
+    strips = [
+        jnp.concatenate(
+            [
+                tap(kernel, ex, rim - y, ez, rows, flip) if 0 <= rim - y < 3 else zero
+                for ez in range(3)
+                for y in range(ys)
+            ],
+            axis=1,
+        )
+        for ex in range(3)
+        for rim in range(ys + 2)
+    ]
+    size = 3 * ys * columns
+    row = lax.broadcasted_iota(jnp.int32, (size, size), 0)
+    column = lax.broadcasted_iota(jnp.int32, (size, size), 1)
+    eye = jnp.where(row == column, 1.0, 0.0).astype(BF)
+    out[...] = lax.dot_general(
+        eye,
+        jnp.concatenate(strips, axis=0),
+        (((1,), (1,)), ((), ())),
+        preferred_element_type=F32,
+    ).astype(BF)
+
+
+def direct(out, kernel, ys, rows, columns, flip):
+    zero = jnp.zeros((rows, columns), BF)
+    for ez in range(3):
+        for y in range(ys):
+            place = (ez * ys + y) * rows
+            out[place : place + rows, :] = jnp.concatenate(
+                [
+                    tap(kernel, ex, rim - y, ez, rows, flip) if 0 <= rim - y < 3 else zero
+                    for ex in range(3)
+                    for rim in range(ys + 2)
+                ],
+                axis=1,
+            )
+
+
 def body(
     wide_count, narrow_count, xs, ys, chans,
-    vol, cot, w_first, w_second, w_bottom, lift, lift_t, w_decode, w_final,
+    vol_in, cot_in, first_in, second_in, bottom_in, lift_in, decode_in, final_in,
+    features_ref, grad_ref,
+    vol, cot, first, second, bottom, lift, decode, final,
+    w_first, w_second, w_bottom, w_decode, w_final,
     b_first, b_second, b_bottom, b_decode, b_final,
-    features_ref, grad_ref,
     e_vol, e_cot, e_p1, e_p2, e_j2, e_j1, e_gd, e_gb, e_gs, e_gf,
     pre_first, hidden_first, grad_joined, pre_second, hidden_second,
-    send_sem, recv_sem,
+    send_sem, recv_sem, load_sem,
 ):
+    loads = [
+        pltpu.make_async_copy(source, target, load_sem.at[place])
+        for place, (source, target) in enumerate(
+            (
+                (vol_in, vol), (cot_in, cot), (first_in, first), (final_in, final),
+                (second_in, second), (bottom_in, bottom), (lift_in, lift), (decode_in, decode),
+            )
+        )
+    ]
+    for load in loads:
+        load.start()
     c1, c2, c3 = chans
     x2, y2 = xs // 2, ys // 2
     x3, y3 = x2 // 2, y2 // 2
@@ -179,8 +239,11 @@
                 device_id_type=pl.DeviceIdType.MESH,
             )
 
-    put(e_vol, [vol[x] for x in range(xs)], c1)
-    put(e_cot, [cot[x] for x in range(xs)], c1)
+    for load, source, edged in ((loads[0], vol, e_vol), (loads[1], cot, e_cot)):
+        load.wait()
+        for x in range(xs):
+            for y in range(ys):
+                edged[x + 1, (y + 1) * c1 : (y + 2) * c1, :] = source[:, x, y, :]
     across = 1 + (me_wide > 0).astype(jnp.int32) + (me_wide < wide_count - 1).astype(jnp.int32)
     along = 1 + (me_narrow > 0).astype(jnp.int32) + (me_narrow < narrow_count - 1).astype(jnp.int32)
     pl.semaphore_wait(barrier, across * along - 1)
@@ -188,6 +251,8 @@
     send(*spec_vol)
     send(*spec_cot)
 
+    loads[2].wait()
+    turned(w_first, first, ys, c1, c1, False)
     receive(*spec_vol)
     hidden = []
     for x, pre in enumerate(conv(w_first, e_vol, xs, 1)):
@@ -198,12 +263,16 @@
     put(e_p1, [p * 0.125 for p in pooled], c1)
     send(*spec_p1)
 
+    loads[3].wait()
+    direct(b_final, final, ys, c1, c1, True)
     receive(*spec_cot)
     joined = [g.astype(BF) for g in conv(b_final, e_cot, xs, 1)]
     for x in range(xs):
         grad_joined[x] = joined[x]
     joined_sum = block_sum([g.astype(F32) for g in joined], c1, 1)
 
+    loads[4].wait()
+    turned(w_second, second, y2, c1, c2, False)
     receive(*spec_p1)
     hidden = []
     for x, pre in enumerate(conv(w_second, e_p1, x2, 2)):
@@ -214,6 +283,9 @@
     put(e_p2, [p * 0.125 for p in pooled], c2)
     send(*spec_p2)
 
+    loads[5].wait()
+    loads[6].wait()
+    turned(w_bottom, bottom, y3, c2, c3, False)
     receive(*spec_p2)
     pre_bottom = conv(w_bottom, e_p2, x3, 4)
     lifted = []
@@ -232,6 +304,8 @@
     put(e_j2, [lifted[x] + hidden_second[x].astype(F32) for x in range(x2)], c2)
     send(*spec_j2)
 
+    loads[7].wait()
+    direct(w_decode, decode, y2, c1, c2, False)
     receive(*spec_j2)
     pre_decode = conv(w_decode, e_j2, x2, 2)
     put(e_gd, [joined_sum[x] * slope(pre_decode[x]) for x in range(x2)], c1)
@@ -240,6 +314,8 @@
     put(e_j1, [decoded[x] + hidden_first[x].astype(F32) for x in range(xs)], c1)
     send(*spec_j1)
 
+    turned(b_decode, decode, y2, c1, c2, True)
+    turned(w_final, final, ys, c1, c1, False)
     receive(*spec_gd)
     second_up = [g.astype(BF).astype(F32) for g in conv(b_decode, e_gd, x2, 2)]
     grad_lift = [g.astype(BF) for g in block_sum(second_up, c2, 2)]
@@ -247,9 +323,10 @@
     for x in range(x3):
         back = jnp.concatenate(
             [
-                jnp.dot(
-                    lift_t[...],
+                lax.dot_general(
+                    lift[...],
                     grad_lift[x][y * c2 : (y + 1) * c2],
+                    (((0,), (0,)), ((), ())),
                     preferred_element_type=F32,
                 )
                 for y in range(y3)
@@ -264,6 +341,7 @@
     for x, out in enumerate(conv(w_final, e_j1, xs, 1)):
         features_ref[x] = out.astype(BF)
 
+    direct(b_bottom, bottom, y3, c2, c3, True)
     receive(*spec_gb)
     pool_second = spread(conv(b_bottom, e_gb, x3, 4), c2)
     put(
@@ -273,6 +351,7 @@
     )
     send(*spec_gs)
 
+    direct(b_second, second, y2, c1, c2, True)
     receive(*spec_gs)
     pool_first = spread(conv(b_second, e_gs, x2, 2), c1)
     put(
@@ -285,6 +364,7 @@
     )
     send(*spec_gf)
 
+    direct(b_first, first, ys, c1, c1, True)
     receive(*spec_gf)
     for x, out in enumerate(conv(b_first, e_gf, xs, 1)):
         grad_ref[x] = out.astype(BF)
@@ -293,23 +373,6 @@
         for side, (dx, dy) in enumerate(SIDES):
             copy = copy_of(index, edged, side, nx, ny, width)
             pl.when(exists(dx, dy))(copy.wait_send)
-
-
-def flipped(kernel):
-    return jnp.flip(kernel, (0, 1, 2)).transpose(0, 1, 2, 4, 3)
-
-
-def banded(kernel, ys):
-    outs, ins = kernel.shape[4], kernel.shape[3]
-    turned = kernel.transpose(2, 4, 0, 1, 3)
-    stacked = jnp.stack(
-        [
-            jnp.pad(turned, ((0, 0), (0, 0), (0, 0), (y, ys - 1 - y), (0, 0)))
-            for y in range(ys)
-        ],
-        axis=1,
-    )
-    return stacked.reshape(3 * ys * outs, 3 * (ys + 2) * ins)
 
 
 def shards(
@@ -320,23 +383,39 @@
     c2, c3 = lift_weight.shape
     x2, y2, x3, y3 = xs // 2, ys // 2, xs // 4, ys // 4
 
-    def columns(field):
-        return field.transpose(1, 2, 0, 3).reshape(xs, ys * c1, lanes)
-
     def back(field):
         return field.reshape(xs, ys, c1, lanes).transpose(2, 0, 1, 3)
 
     def edged(nx, ny, width):
         return pltpu.VMEM((nx + 2, (ny + 2) * width, lanes), BF)
 
+    def matrix(count, ins, outs):
+        return pltpu.VMEM((3 * count * outs, 3 * (count + 2) * ins), BF)
+
+    sizes = ((ys, c1, c1), (y2, c1, c2), (y3, c2, c3), (y2, c2, c1), (ys, c1, c1))
+    first, second, bottom, decode, final = (
+        k.reshape(27 * k.shape[3], k.shape[4])
+        for k in (
+            conv_first,
+            conv_second,
+            conv_bottom,
+            conv_decode.transpose(0, 1, 2, 4, 3),
+            conv_final,
+        )
+    )
     shape = jax.ShapeDtypeStruct((xs, ys * c1, lanes), BF)
     vmem = pl.BlockSpec(memory_space=pltpu.VMEM)
     call = pl.pallas_call(
         functools.partial(body, wide_count, narrow_count, xs, ys, (c1, c2, c3)),
         out_shape=(shape, shape),
-        in_specs=[vmem] * 14,
+        in_specs=[pl.BlockSpec(memory_space=pl.ANY)] * 8,
         out_specs=(vmem, vmem),
         scratch_shapes=[
+            pltpu.VMEM(volume.shape, BF),
+            pltpu.VMEM(cotangent.shape, BF),
+            *(pltpu.VMEM(k.shape, BF) for k in (first, second, bottom, lift_weight, decode, final)),
+            *(matrix(n, i, o) for n, i, o in sizes),
+            *(matrix(n, o, i) for n, i, o in sizes),
             edged(xs, ys, c1),
             edged(xs, ys, c1),
             edged(x2, y2, c1),
@@ -354,26 +433,14 @@
             pltpu.VMEM((x2, y2 * c2, lanes), BF),
             pltpu.SemaphoreType.DMA((10, 8)),
             pltpu.SemaphoreType.DMA((10, 8)),
+            pltpu.SemaphoreType.DMA((8,)),
         ],
         compiler_params=pltpu.CompilerParams(
-            collective_id=0, has_side_effects=True, vmem_limit_bytes=40 * 1024 * 1024
+            collective_id=0, has_side_effects=True, vmem_limit_bytes=60 * 1024 * 1024
         ),
     )
     features, grad = call(
-        columns(volume),
-        columns(cotangent),
-        banded(conv_first, ys),
-        banded(conv_second, y2),
-        banded(conv_bottom, y3),
-        lift_weight,
-        lift_weight.T,
-        banded(conv_decode, y2),
-        banded(conv_final, ys),
-        banded(flipped(conv_first), ys),
-        banded(flipped(conv_second), y2),
-        banded(flipped(conv_bottom), y3),
-        banded(flipped(conv_decode), y2),
-        banded(flipped(conv_final), ys),
+        volume, cotangent, first, second, bottom, lift_weight, decode, final
     )
     return back(features), back(grad)
 

time: 88.5 us -> 42.3 us (0.48)
  local copies, waits for them, and re-layouts: 45.6 us -> 1.8 us
  other arithmetic: 2.38 us -> 0 us
    reshape x14 -> x0, local copies, waits for them, and re-layouts: 21.6 us -> none  [banded(): return stacked.reshape(3 * ys * outs, 3 * (ys + 2) * ins)]
    another operation x21 -> x0, local copies, waits for them, and re-layouts: 16.1 us -> none  [the longest x3 7.28 us: banded(): return stacked.reshape(3 * ys * outs, 3 * (ys + 2) * ins)]
    unnamed x23 -> x0, local copies, waits for them, and re-layouts: 3.88 us -> none
    transpose x2 -> x0, local copies, waits for them, and re-layouts: 3.19 us -> none  [columns(): return field.transpose(1, 2, 0, 3).reshape(xs, ys * c1, lanes)]
    another operation x8 -> x0, other arithmetic: 2.38 us -> none  [banded(): jnp.stack([jnp.pad(turned, ((0, 0), (0, 0), (0, 0), (y, ys - 1 - y), (0,...]
    transpose x1, local copies, waits for them, and re-layouts: 0.83 us -> 1.8 us  [back(): return field.reshape(xs, ys, c1, lanes).transpose(2, 0, 1, 3)]
where the time goes in v3:
time: 42.3 us; the launch traced here: 41.9 us
  Pallas kernels  39.5 us (93%)
  local copies, waits for them, and re-layouts  1.8 us (4%)
  between operations  0.64 us (2%)
    pallas_call x1, Pallas kernels, shards(): call(volume, cotangent, first, second, bottom, lift_weight, decode, final)  39.5 us
    transpose x1, local copies, waits for them, and re-layouts, back(): return field.reshape(xs, ys, c1, lanes).transpose(2, 0, 1, 3)  1.8 us

profile of v3, /device:TPU:4, one launch (start us, length us, event | category | flops | bytes accessed | tf_op | source)
XLA Modules:
  0.0 41.9 jit_solution(13835564718649893130)
XLA Ops:
  0.6 39.5 %shard_map.95 = (bf16[4,128,128]{2,1,0:T(8,128)(2,1)}, bf16[4,128,128]{2,1,0:T(8,128)(2,1)}) custom-call(bf16[32,4,4,128]{3,2,1,0:T(4,128)(2,1)} %vol_in.1, bf16[32,4,4,128]{3,2,1,0:T(4,128)(2,1)} %cot_in.1, bf16[864,32]{1,0:T(8,128)(2,1)} %bitcast.14, bf16[864,64]{1,0:T(8,128)(2,1)} %bitcast.15, bf16[1728,128]{1,0:T(8,128)(2,1)} %bitcast.13, ...), custom_call_target="tpu_custom_call" | custom-call | tf_op jit(solution)/shard_map/pallas_call | solution.py:442
  40.1 1.8 %copy_bitcast_fusion = (bf16[32,4,4,128]{3,2,1,0:T(4,128)(2,1)}, bf16[32,4,4,128]{3,2,1,0:T(4,128)(2,1)}) fusion(bf16[4,4,32,128]{3,2,1,0:T(8,128)(2,1)} %bitcast.19, bf16[4,4,32,128]{3,2,1,0:T(8,128)(2,1)} %bitcast.18), kind=kLoop, calls=%fused_computation | loop fusion | bytes 524288 | tf_op jit(solution)/shard_map/transpose | solution.py:387

commit v4 on v3

--- a/solution.py
+++ b/solution.py
@@ -135,8 +135,8 @@
     vol, cot, first, second, bottom, lift, decode, final,
     w_first, w_second, w_bottom, w_decode, w_final,
     b_first, b_second, b_bottom, b_decode, b_final,
-    e_vol, e_cot, e_p1, e_p2, e_j2, e_j1, e_gd, e_gb, e_gs, e_gf,
-    pre_first, hidden_first, grad_joined, pre_second, hidden_second,
+    e_vol, e_cot, e_p1, e_p2, e_j2, e_j1, e_gd, e_gb, e_gs, e_gf, e_js, e_gj, e_sl,
+    hidden_first, pre_second, hidden_second,
     send_sem, recv_sem, load_sem,
 ):
     loads = [
@@ -162,19 +162,19 @@
             (near_x >= 0) & (near_x < wide_count) & (near_y >= 0) & (near_y < narrow_count)
         )
 
-    def span(delta, count, sending):
+    def span(delta, count, halo, sending):
         if delta == 0:
-            return 1, count
+            return halo, count
         if sending:
-            return (count if delta > 0 else 1), 1
-        return (0 if delta > 0 else count + 1), 1
-
-    def copy_of(index, edged, side, nx, ny, width):
+            return (count if delta > 0 else halo), halo
+        return (0 if delta > 0 else count + halo), halo
+
+    def copy_of(index, edged, side, nx, ny, width, halo):
         dx, dy = SIDES[side]
 
         def part(sending):
-            x_at, x_len = span(dx, nx, sending)
-            y_at, y_len = span(dy, ny, sending)
+            x_at, x_len = span(dx, nx, halo, sending)
+            y_at, y_len = span(dy, ny, halo, sending)
             return edged.at[pl.ds(x_at, x_len), pl.ds(y_at * width, y_len * width), :]
 
         return pltpu.make_async_remote_copy(
@@ -188,42 +188,47 @@
 
     started = []
 
-    def send(index, edged, nx, ny, width):
+    def send(*spec):
         for side, (dx, dy) in enumerate(SIDES):
-            copy = copy_of(index, edged, side, nx, ny, width)
+            copy = copy_of(*spec[:2], side, *spec[2:])
             pl.when(exists(dx, dy))(copy.start)
-        started.append((index, edged, nx, ny, width))
-
-    def receive(index, edged, nx, ny, width):
+        started.append(spec)
+
+    def receive(*spec):
         for side, (dx, dy) in enumerate(SIDES):
-            copy = copy_of(index, edged, side, nx, ny, width)
+            copy = copy_of(*spec[:2], side, *spec[2:])
             pl.when(exists(-dx, -dy))(copy.wait_recv)
 
-    def put(edged, fields, width):
+    def put(edged, fields, width, halo=1):
         rows = fields[0].shape[0]
         for x, field in enumerate(fields):
-            edged[x + 1, width : width + rows, :] = field.astype(BF)
-
-    def clear(edged, nx, ny, width):
+            edged[x + halo, halo * width : halo * width + rows, :] = field.astype(edged.dtype)
+
+    def clear(edged, nx, ny, width, halo):
         lanes = edged.shape[2]
-        edged[0] = jnp.zeros(((ny + 2) * width, lanes), BF)
-        edged[nx + 1] = jnp.zeros(((ny + 2) * width, lanes), BF)
-        for x in range(1, nx + 1):
-            edged[x, 0:width, :] = jnp.zeros((width, lanes), BF)
-            edged[x, (ny + 1) * width : (ny + 2) * width, :] = jnp.zeros((width, lanes), BF)
-
-    spec_vol = (0, e_vol, xs, ys, c1)
-    spec_cot = (1, e_cot, xs, ys, c1)
-    spec_p1 = (2, e_p1, x2, y2, c1)
-    spec_p2 = (3, e_p2, x3, y3, c2)
-    spec_j2 = (4, e_j2, x2, y2, c2)
-    spec_j1 = (5, e_j1, xs, ys, c1)
-    spec_gd = (6, e_gd, x2, y2, c1)
-    spec_gb = (7, e_gb, x3, y3, c3)
-    spec_gs = (8, e_gs, x2, y2, c2)
-    spec_gf = (9, e_gf, xs, ys, c1)
+        whole = jnp.zeros(((ny + 2 * halo) * width, lanes), edged.dtype)
+        rim = jnp.zeros((halo * width, lanes), edged.dtype)
+        for x in range(halo):
+            edged[x] = whole
+            edged[nx + halo + x] = whole
+        for x in range(halo, nx + halo):
+            edged[x, 0 : halo * width, :] = rim
+            edged[x, (ny + halo) * width : (ny + 2 * halo) * width, :] = rim
+
+    spec_vol = (0, e_vol, xs, ys, c1, 1)
+    spec_cot = (1, e_cot, xs, ys, c1, 1)
+    spec_p1 = (2, e_p1, x2, y2, c1, 1)
+    spec_p2 = (3, e_p2, x3, y3, c2, 1)
+    spec_j2 = (4, e_j2, x2, y2, c2, 2)
+    spec_j1 = (5, e_j1, xs, ys, c1, 1)
+    spec_js = (6, e_js, x2, y2, c1, 1)
+    spec_gb = (7, e_gb, x3, y3, c3, 1)
+    spec_gs = (8, e_gs, x2, y2, c2, 2)
+    spec_gj = (9, e_gj, xs, ys, c1, 1)
+    spec_sl = (10, e_sl, xs, ys, c1, 1)
     for spec in (
-        spec_vol, spec_cot, spec_p1, spec_p2, spec_j2, spec_j1, spec_gd, spec_gb, spec_gs, spec_gf
+        spec_vol, spec_cot, spec_p1, spec_p2, spec_j2, spec_j1, spec_js, spec_gb, spec_gs,
+        spec_gj, spec_sl,
     ):
         clear(*spec[1:])
 
@@ -254,22 +259,25 @@
     loads[2].wait()
     turned(w_first, first, ys, c1, c1, False)
     receive(*spec_vol)
-    hidden = []
+    hidden, slopes = [], []
     for x, pre in enumerate(conv(w_first, e_vol, xs, 1)):
-        pre_first[x] = pre
+        slopes.append(slope(pre))
         hidden.append(silu(pre).astype(BF))
         hidden_first[x] = hidden[-1]
     pooled = block_sum([h.astype(F32) for h in hidden], c1, 1)
     put(e_p1, [p * 0.125 for p in pooled], c1)
     send(*spec_p1)
+    put(e_sl, slopes, c1)
+    send(*spec_sl)
 
     loads[3].wait()
     direct(b_final, final, ys, c1, c1, True)
     receive(*spec_cot)
     joined = [g.astype(BF) for g in conv(b_final, e_cot, xs, 1)]
-    for x in range(xs):
-        grad_joined[x] = joined[x]
-    joined_sum = block_sum([g.astype(F32) for g in joined], c1, 1)
+    put(e_gj, joined, c1)
+    put(e_js, block_sum([g.astype(F32) for g in joined], c1, 1), c1)
+    send(*spec_js)
+    send(*spec_gj)
 
     loads[4].wait()
     turned(w_second, second, y2, c1, c2, False)
@@ -301,22 +309,22 @@
             )
         )
     lifted = spread(lifted, c2)
-    put(e_j2, [lifted[x] + hidden_second[x].astype(F32) for x in range(x2)], c2)
+    put(e_j2, [lifted[x] + hidden_second[x].astype(F32) for x in range(x2)], c2, 2)
     send(*spec_j2)
 
     loads[7].wait()
-    direct(w_decode, decode, y2, c1, c2, False)
+    direct(w_decode, decode, y2 + 2, c1, c2, False)
+    turned(b_decode, decode, y2, c1, c2, True)
     receive(*spec_j2)
-    pre_decode = conv(w_decode, e_j2, x2, 2)
-    put(e_gd, [joined_sum[x] * slope(pre_decode[x]) for x in range(x2)], c1)
-    send(*spec_gd)
-    decoded = spread([silu(pre).astype(BF).astype(F32) for pre in pre_decode], c1)
+    pre_decode = conv(w_decode, e_j2, x2 + 2, 2)
+    inner = [pre[c1 : (y2 + 1) * c1] for pre in pre_decode[1:-1]]
+    decoded = spread([silu(pre).astype(BF).astype(F32) for pre in inner], c1)
     put(e_j1, [decoded[x] + hidden_first[x].astype(F32) for x in range(xs)], c1)
     send(*spec_j1)
 
-    turned(b_decode, decode, y2, c1, c2, True)
-    turned(w_final, final, ys, c1, c1, False)
-    receive(*spec_gd)
+    receive(*spec_js)
+    for x in range(x2 + 2):
+        e_gd[x] = (e_js[x] * slope(pre_decode[x])).astype(BF)
     second_up = [g.astype(BF).astype(F32) for g in conv(b_decode, e_gd, x2, 2)]
     grad_lift = [g.astype(BF) for g in block_sum(second_up, c2, 2)]
     grad_bottom = []
@@ -337,6 +345,7 @@
     put(e_gb, grad_bottom, c3)
     send(*spec_gb)
 
+    turned(w_final, final, ys, c1, c1, False)
     receive(*spec_j1)
     for x, out in enumerate(conv(w_final, e_j1, xs, 1)):
         features_ref[x] = out.astype(BF)
@@ -348,30 +357,25 @@
         e_gs,
         [(second_up[x] + pool_second[x] * 0.125) * slope(pre_second[x]) for x in range(x2)],
         c2,
+        2,
     )
     send(*spec_gs)
 
-    direct(b_second, second, y2, c1, c2, True)
+    direct(b_second, second, y2 + 2, c1, c2, True)
+    direct(b_first, first, ys, c1, c1, True)
     receive(*spec_gs)
-    pool_first = spread(conv(b_second, e_gs, x2, 2), c1)
-    put(
-        e_gf,
-        [
-            (grad_joined[x].astype(F32) + pool_first[x] * 0.125) * slope(pre_first[x])
-            for x in range(xs)
-        ],
-        c1,
-    )
-    send(*spec_gf)
-
-    direct(b_first, first, ys, c1, c1, True)
-    receive(*spec_gf)
+    pool_first = spread(conv(b_second, e_gs, x2 + 2, 2), c1)
+    receive(*spec_gj)
+    receive(*spec_sl)
+    for x in range(xs + 2):
+        lower = pool_first[x + 1][c1 : (ys + 3) * c1]
+        e_gf[x] = ((e_gj[x].astype(F32) + lower * 0.125) * e_sl[x]).astype(BF)
     for x, out in enumerate(conv(b_first, e_gf, xs, 1)):
         grad_ref[x] = out.astype(BF)
 
-    for index, edged, nx, ny, width in started:
+    for spec in started:
         for side, (dx, dy) in enumerate(SIDES):
-            copy = copy_of(index, edged, side, nx, ny, width)
+            copy = copy_of(*spec[:2], side, *spec[2:])
             pl.when(exists(dx, dy))(copy.wait_send)
 
 
@@ -386,13 +390,12 @@
     def back(field):
         return field.reshape(xs, ys, c1, lanes).transpose(2, 0, 1, 3)
 
-    def edged(nx, ny, width):
-        return pltpu.VMEM((nx + 2, (ny + 2) * width, lanes), BF)
+    def edged(nx, ny, width, halo=1, kind=BF):
+        return pltpu.VMEM((nx + 2 * halo, (ny + 2 * halo) * width, lanes), kind)
 
     def matrix(count, ins, outs):
         return pltpu.VMEM((3 * count * outs, 3 * (count + 2) * ins), BF)
 
-    sizes = ((ys, c1, c1), (y2, c1, c2), (y3, c2, c3), (y2, c2, c1), (ys, c1, c1))
     first, second, bottom, decode, final = (
         k.reshape(27 * k.shape[3], k.shape[4])
         for k in (
@@ -414,25 +417,34 @@
             pltpu.VMEM(volume.shape, BF),
             pltpu.VMEM(cotangent.shape, BF),
             *(pltpu.VMEM(k.shape, BF) for k in (first, second, bottom, lift_weight, decode, final)),
-            *(matrix(n, i, o) for n, i, o in sizes),
-            *(matrix(n, o, i) for n, i, o in sizes),
+            matrix(ys, c1, c1),
+            matrix(y2, c1, c2),
+            matrix(y3, c2, c3),
+            matrix(y2 + 2, c2, c1),
+            matrix(ys, c1, c1),
+            matrix(ys, c1, c1),
+            matrix(y2 + 2, c2, c1),
+            matrix(y3, c3, c2),
+            matrix(y2, c1, c2),
+            matrix(ys, c1, c1),
             edged(xs, ys, c1),
             edged(xs, ys, c1),
             edged(x2, y2, c1),
             edged(x3, y3, c2),
-            edged(x2, y2, c2),
+            edged(x2, y2, c2, 2),
             edged(xs, ys, c1),
             edged(x2, y2, c1),
             edged(x3, y3, c3),
-            edged(x2, y2, c2),
+            edged(x2, y2, c2, 2),
             edged(xs, ys, c1),
-            pltpu.VMEM((xs, ys * c1, lanes), F32),
-            pltpu.VMEM((xs, ys * c1, lanes), BF),
+            edged(x2, y2, c1, 1, F32),
+            edged(xs, ys, c1),
+            edged(xs, ys, c1, 1, F32),
             pltpu.VMEM((xs, ys * c1, lanes), BF),
             pltpu.VMEM((x2, y2 * c2, lanes), F32),
             pltpu.VMEM((x2, y2 * c2, lanes), BF),
-            pltpu.SemaphoreType.DMA((10, 8)),
-            pltpu.SemaphoreType.DMA((10, 8)),
+            pltpu.SemaphoreType.DMA((11, 8)),
+            pltpu.SemaphoreType.DMA((11, 8)),
             pltpu.SemaphoreType.DMA((8,)),
         ],
         compiler_params=pltpu.CompilerParams(

time: 42.3 us -> 43.5 us (1.028)
  Pallas kernels: 39.5 us -> 40.6 us
    pallas_call x1, Pallas kernels: 39.5 us -> 40.6 us  [shards(): call(volume, cotangent, first, second, bottom, lift_weight, decode, final)]
where the time goes in v4:
time: 43.5 us; the launch traced here: 43 us
  Pallas kernels  40.6 us (93%)
  local copies, waits for them, and re-layouts  1.8 us (4%)
  between operations  0.64 us (1%)
    pallas_call x1, Pallas kernels, shards(): call(volume, cotangent, first, second, bottom, lift_weight, decode, final)  40.6 us
    transpose x1, local copies, waits for them, and re-layouts, back(): return field.reshape(xs, ys, c1, lanes).transpose(2, 0, 1, 3)  1.8 us

profile of v4, /device:TPU:4, one launch (start us, length us, event | category | flops | bytes accessed | tf_op | source)
XLA Modules:
  0.0 43.0 jit_solution(14442232984308331298)
XLA Ops:
  0.6 40.6 %shard_map.95 = (bf16[4,128,128]{2,1,0:T(8,128)(2,1)}, bf16[4,128,128]{2,1,0:T(8,128)(2,1)}) custom-call(bf16[32,4,4,128]{3,2,1,0:T(4,128)(2,1)} %vol_in.1, bf16[32,4,4,128]{3,2,1,0:T(4,128)(2,1)} %cot_in.1, bf16[864,32]{1,0:T(8,128)(2,1)} %bitcast.14, bf16[864,64]{1,0:T(8,128)(2,1)} %bitcast.15, bf16[1728,128]{1,0:T(8,128)(2,1)} %bitcast.13, ...), custom_call_target="tpu_custom_call" | custom-call | tf_op jit(solution)/shard_map/pallas_call | solution.py:454
  41.2 1.8 %copy_bitcast_fusion = (bf16[32,4,4,128]{3,2,1,0:T(4,128)(2,1)}, bf16[32,4,4,128]{3,2,1,0:T(4,128)(2,1)}) fusion(bf16[4,4,32,128]{3,2,1,0:T(8,128)(2,1)} %bitcast.19, bf16[4,4,32,128]{3,2,1,0:T(8,128)(2,1)} %bitcast.18), kind=kLoop, calls=%fused_computation | loop fusion | bytes 524288 | tf_op jit(solution)/shard_map/transpose | solution.py:391

commit v5 on v4

--- a/solution.py
+++ b/solution.py
@@ -35,10 +35,13 @@
     rows = weights.shape[0] // 3
     matrix = weights[...]
     outs = []
-    for x in range(xs):
-        part = jnp.dot(
-            matrix, edged[x : x + 3].reshape(depth, lanes), preferred_element_type=F32
-        )
+    parts = []
+    for first in range(0, xs, 2):
+        group = range(first, min(first + 2, xs))
+        wide = jnp.concatenate([edged[x : x + 3].reshape(depth, lanes) for x in group], axis=1)
+        both = jnp.dot(matrix, wide, preferred_element_type=F32)
+        parts += [both[:, place * lanes : (place + 1) * lanes] for place in range(len(group))]
+    for part in parts:
         low, mid, high = part[:rows], part[rows : 2 * rows], part[2 * rows :]
         lane = lane_of(low)
         low = jnp.where(lane < step, 0.0, pltpu.roll(low, step, 1))

time: 43.5 us -> 42.5 us (0.977)
  Pallas kernels: 40.6 us -> 39.6 us
    pallas_call x1, Pallas kernels: 40.6 us -> 39.6 us  [shards(): call(volume, cotangent, first, second, bottom, lift_weight, decode, final)]
where the time goes in v5:
time: 42.5 us; the launch traced here: 42 us
  Pallas kernels  39.6 us (93%)
  local copies, waits for them, and re-layouts  1.8 us (4%)
  between operations  0.64 us (2%)
    pallas_call x1, Pallas kernels, shards(): call(volume, cotangent, first, second, bottom, lift_weight, decode, final)  39.6 us
    transpose x1, local copies, waits for them, and re-layouts, back(): return field.reshape(xs, ys, c1, lanes).transpose(2, 0, 1, 3)  1.8 us

profile of v5, /device:TPU:4, one launch (start us, length us, event | category | flops | bytes accessed | tf_op | source)
XLA Modules:
  0.0 42.0 jit_solution(16354044056601517047)
XLA Ops:
  0.6 39.6 %shard_map.95 = (bf16[4,128,128]{2,1,0:T(8,128)(2,1)}, bf16[4,128,128]{2,1,0:T(8,128)(2,1)}) custom-call(bf16[32,4,4,128]{3,2,1,0:T(4,128)(2,1)} %vol_in.1, bf16[32,4,4,128]{3,2,1,0:T(4,128)(2,1)} %cot_in.1, bf16[864,32]{1,0:T(8,128)(2,1)} %bitcast.14, bf16[864,64]{1,0:T(8,128)(2,1)} %bitcast.15, bf16[1728,128]{1,0:T(8,128)(2,1)} %bitcast.13, ...), custom_call_target="tpu_custom_call" | custom-call | tf_op jit(solution)/shard_map/pallas_call | solution.py:457
  40.2 1.8 %copy_bitcast_fusion = (bf16[32,4,4,128]{3,2,1,0:T(4,128)(2,1)}, bf16[32,4,4,128]{3,2,1,0:T(4,128)(2,1)}) fusion(bf16[4,4,32,128]{3,2,1,0:T(8,128)(2,1)} %bitcast.19, bf16[4,4,32,128]{3,2,1,0:T(8,128)(2,1)} %bitcast.18), kind=kLoop, calls=%fused_computation | loop fusion | bytes 524288 | tf_op jit(solution)/shard_map/transpose | solution.py:394

commit v6 on v3

--- a/solution.py
+++ b/solution.py
@@ -35,10 +35,13 @@
     rows = weights.shape[0] // 3
     matrix = weights[...]
     outs = []
-    for x in range(xs):
-        part = jnp.dot(
-            matrix, edged[x : x + 3].reshape(depth, lanes), preferred_element_type=F32
-        )
+    parts = []
+    for first in range(0, xs, 2):
+        group = range(first, min(first + 2, xs))
+        wide = jnp.concatenate([edged[x : x + 3].reshape(depth, lanes) for x in group], axis=1)
+        both = jnp.dot(matrix, wide, preferred_element_type=F32)
+        parts += [both[:, place * lanes : (place + 1) * lanes] for place in range(len(group))]
+    for part in parts:
         low, mid, high = part[:rows], part[rows : 2 * rows], part[2 * rows :]
         lane = lane_of(low)
         low = jnp.where(lane < step, 0.0, pltpu.roll(low, step, 1))
@@ -194,7 +197,15 @@
             pl.when(exists(dx, dy))(copy.start)
         started.append((index, edged, nx, ny, width))
 
+    def drain(keep):
+        while len(started) > keep:
+            index, edged, nx, ny, width = started.pop(0)
+            for side, (dx, dy) in enumerate(SIDES):
+                copy = copy_of(index, edged, side, nx, ny, width)
+                pl.when(exists(dx, dy))(copy.wait_send)
+
     def receive(index, edged, nx, ny, width):
+        drain(2)
         for side, (dx, dy) in enumerate(SIDES):
             copy = copy_of(index, edged, side, nx, ny, width)
             pl.when(exists(-dx, -dy))(copy.wait_recv)
@@ -369,10 +380,7 @@
     for x, out in enumerate(conv(b_first, e_gf, xs, 1)):
         grad_ref[x] = out.astype(BF)
 
-    for index, edged, nx, ny, width in started:
-        for side, (dx, dy) in enumerate(SIDES):
-            copy = copy_of(index, edged, side, nx, ny, width)
-            pl.when(exists(dx, dy))(copy.wait_send)
+    drain(0)
 
 
 def shards(

time: 42.3 us -> 41.9 us (level)
  no operation moved by 1% of the time
where the time goes in v6:
time: 41.9 us; the launch traced here: 41.6 us
  Pallas kernels  39.1 us (93%)
  local copies, waits for them, and re-layouts  1.8 us (4%)
  between operations  0.64 us (2%)
    pallas_call x1, Pallas kernels, shards(): call(volume, cotangent, first, second, bottom, lift_weight, decode, final)  39.1 us
    transpose x1, local copies, waits for them, and re-layouts, back(): return field.reshape(xs, ys, c1, lanes).transpose(2, 0, 1, 3)  1.8 us

profile of v6, /device:TPU:4, one launch (start us, length us, event | category | flops | bytes accessed | tf_op | source)
XLA Modules:
  0.0 41.6 jit_solution(614925302796563996)
XLA Ops:
  0.6 39.1 %shard_map.95 = (bf16[4,128,128]{2,1,0:T(8,128)(2,1)}, bf16[4,128,128]{2,1,0:T(8,128)(2,1)}) custom-call(bf16[32,4,4,128]{3,2,1,0:T(4,128)(2,1)} %vol_in.1, bf16[32,4,4,128]{3,2,1,0:T(4,128)(2,1)} %cot_in.1, bf16[864,32]{1,0:T(8,128)(2,1)} %bitcast.14, bf16[864,64]{1,0:T(8,128)(2,1)} %bitcast.15, bf16[1728,128]{1,0:T(8,128)(2,1)} %bitcast.13, ...), custom_call_target="tpu_custom_call" | custom-call | tf_op jit(solution)/shard_map/pallas_call | solution.py:450
  39.8 1.8 %copy_bitcast_fusion = (bf16[32,4,4,128]{3,2,1,0:T(4,128)(2,1)}, bf16[32,4,4,128]{3,2,1,0:T(4,128)(2,1)}) fusion(bf16[4,4,32,128]{3,2,1,0:T(8,128)(2,1)} %bitcast.19, bf16[4,4,32,128]{3,2,1,0:T(8,128)(2,1)} %bitcast.18), kind=kLoop, calls=%fused_computation | loop fusion | bytes 524288 | tf_op jit(solution)/shard_map/transpose | solution.py:395

commit v7 on v6

--- a/solution.py
+++ b/solution.py
@@ -9,7 +9,7 @@
 
 BF = jnp.bfloat16
 F32 = jnp.float32
-SIDES = tuple((dx, dy) for dx in (-1, 0, 1) for dy in (-1, 0, 1) if (dx, dy) != (0, 0))
+SIDES = ((-1, -1), (-1, 1), (1, -1), (1, 1), (-1, 0), (1, 0), (0, -1), (0, 1))
 
 
 def sigmoid(value):
@@ -250,16 +250,19 @@
                 device_id_type=pl.DeviceIdType.MESH,
             )
 
-    for load, source, edged in ((loads[0], vol, e_vol), (loads[1], cot, e_cot)):
+    def place_columns(load, source, edged):
         load.wait()
         for x in range(xs):
             for y in range(ys):
                 edged[x + 1, (y + 1) * c1 : (y + 2) * c1, :] = source[:, x, y, :]
+
+    place_columns(loads[0], vol, e_vol)
     across = 1 + (me_wide > 0).astype(jnp.int32) + (me_wide < wide_count - 1).astype(jnp.int32)
     along = 1 + (me_narrow > 0).astype(jnp.int32) + (me_narrow < narrow_count - 1).astype(jnp.int32)
     pl.semaphore_wait(barrier, across * along - 1)
 
     send(*spec_vol)
+    place_columns(loads[1], cot, e_cot)
     send(*spec_cot)
 
     loads[2].wait()

time: 41.9 us -> 41.5 us (level)
  the two profiles are of different devices: /device:TPU:4 before, /device:TPU:1 now
where the time goes in v7:
time: 41.5 us; the launch traced here: 41.3 us
  Pallas kernels  38.9 us (94%)
  local copies, waits for them, and re-layouts  1.8 us (4%)
  between operations  0.64 us (2%)
    pallas_call x1, Pallas kernels, shards(): call(volume, cotangent, first, second, bottom, lift_weight, decode, final)  38.9 us
    transpose x1, local copies, waits for them, and re-layouts, back(): return field.reshape(xs, ys, c1, lanes).transpose(2, 0, 1, 3)  1.8 us

profile of v7, /device:TPU:1, one launch (start us, length us, event | category | flops | bytes accessed | tf_op | source)
XLA Modules:
  0.0 41.3 jit_solution(12192511255357460936)
XLA Ops:
  0.6 38.9 %shard_map.95 = (bf16[4,128,128]{2,1,0:T(8,128)(2,1)}, bf16[4,128,128]{2,1,0:T(8,128)(2,1)}) custom-call(bf16[32,4,4,128]{3,2,1,0:T(4,128)(2,1)} %vol_in.1, bf16[32,4,4,128]{3,2,1,0:T(4,128)(2,1)} %cot_in.1, bf16[864,32]{1,0:T(8,128)(2,1)} %bitcast.14, bf16[864,64]{1,0:T(8,128)(2,1)} %bitcast.15, bf16[1728,128]{1,0:T(8,128)(2,1)} %bitcast.13, ...), custom_call_target="tpu_custom_call" | custom-call | tf_op jit(solution)/shard_map/pallas_call | solution.py:453
  39.5 1.8 %copy_bitcast_fusion = (bf16[32,4,4,128]{3,2,1,0:T(4,128)(2,1)}, bf16[32,4,4,128]{3,2,1,0:T(4,128)(2,1)}) fusion(bf16[4,4,32,128]{3,2,1,0:T(8,128)(2,1)} %bitcast.19, bf16[4,4,32,128]{3,2,1,0:T(8,128)(2,1)} %bitcast.18), kind=kLoop, calls=%fused_computation | loop fusion | bytes 524288 | tf_op jit(solution)/shard_map/transpose | solution.py:398
